TPU v7x, 32 devices: a whole 2x2x4 slice. The times are simulated.
32 devices in a mesh: dp: 8 (over y, x, core), blk: 4 (over z).
Axes of the slice: x: 2, y: 2, z: 4, core: 2. Of those that a mesh axis runs over, the one named last changes fastest.
Arguments:
- hidden_in: bfloat16 [2, 8, 1024, 768], P(None, 'dp', 'blk'), may hold values from -6 to 6
- segment_ids: int32 [2, 8, 1024], P(None, 'dp', 'blk'), may hold values from 0 to 15, as said below
- queries: bfloat16 [2, 128, 768], P(None, 'dp'), may hold values from -0.5390625 to 0.5390625
- targets: int32 [2, 128], P(None, 'dp'), may hold values from 0 to 127, each once within a row
- cotangent: bfloat16 [2, 8, 1024, 768], P(None, 'dp', 'blk'), may hold values from -3 to 3
- query_weight: bfloat16 [768, 768], P('dp'), may hold values from -0.21875 to 0.21875
- key_weight: bfloat16 [768, 768], P('dp'), may hold values from -0.21875 to 0.21875
- value_weight: bfloat16 [768, 768], P('dp'), may hold values from -0.21875 to 0.21875
- output_weight: bfloat16 [768, 768], P('dp'), may hold values from -1.75 to 1.75
- query_bias: bfloat16 [768], P('dp'), may hold values from -3 to 3
- value_bias: bfloat16 [768], P('dp'), may hold values from -0.29882812 to 0.29882812
- output_bias: bfloat16 [768], P('dp'), may hold values from -1.1953125 to 1.1953125
- first_gain: bfloat16 [768], P('dp'), may hold values from 0.5 to 1.5
- first_shift: bfloat16 [768], P('dp'), may hold values from -1.1953125 to 1.1953125
- inner_weight: bfloat16 [768, 3072], P('dp'), may hold values from -0.21875 to 0.21875
- inner_bias: bfloat16 [3072], P('dp'), may hold values from -1.796875 to 1.796875
- outer_weight: bfloat16 [3072, 768], P('dp'), may hold values from -0.109375 to 0.109375
- outer_bias: bfloat16 [768], P('dp'), may hold values from -1.1953125 to 1.1953125
- second_gain: bfloat16 [768], P('dp'), may hold values from 0.5 to 1.5
- second_shift: bfloat16 [768], P('dp'), may hold values from -1.1953125 to 1.1953125
Outputs:
- hidden_out: bfloat16 [2, 8, 1024, 768], P(None, 'dp', 'blk')
- embeddings: bfloat16 [2, 128, 768], P(None, 'dp')
- query_loss: float32 [2, 128], P(None, 'dp')
- query_grad: float32 [2, 128, 768], P(None, 'dp')
- hidden_grad: bfloat16 [2, 8, 1024, 768], P(None, 'dp', 'blk')
- query_weight_grad: float32 [768, 768], P('dp')
- key_weight_grad: float32 [768, 768], P('dp')
- value_weight_grad: float32 [768, 768], P('dp')
- output_weight_grad: float32 [768, 768], P('dp')
- query_bias_grad: float32 [768], P('dp')
- value_bias_grad: float32 [768], P('dp')
- output_bias_grad: float32 [768], P('dp')
- first_gain_grad: float32 [768], P('dp')
- first_shift_grad: float32 [768], P('dp')
- inner_weight_grad: float32 [768, 3072], P('dp')
- inner_bias_grad: float32 [3072], P('dp')
- outer_weight_grad: float32 [3072, 768], P('dp')
- outer_bias_grad: float32 [768], P('dp')
- second_gain_grad: float32 [768], P('dp')
- second_shift_grad: float32 [768], P('dp')
Inputs may be any that keep to these rules, and one draw needn't show every extreme that they name: `segment_ids`: in each row the segment numbers never fall along the row and every number occurs; the first position of a segment is its CLS token. For each index of dp, one of its rows in one of the micro-batches holds a segment that begins within the first 256 positions and ends within the last 256; in every other row each block of 256 positions holds the first positions of exactly 4 segments. Each micro-batch's targets name every passage of it once.
All inputs are finite; a program needn't handle non-finite values.
Results may differ from a plain program's by a relative error of at most 0.023.
Values may be sent and summed in bfloat16 or wider, within the bound.
A program may use at most 80 MiB of HBM per device.

v0:
```python
import math

import jax
import jax.numpy as jnp
from jax import lax
from jax.sharding import PartitionSpec as P

HEADS = 12


EPSILON = 1e-12
NEGATIVE = -1000000000.0
PRECISE = lax.Precision.HIGHEST


def passed_along(x, axis, by):
    size = lax.axis_size(axis)
    return lax.ppermute(x, axis, [(i, (i + by) % size) for i in range(size)])


def as_sent(x):
    return jax.tree.map(lambda a: a.astype(jnp.bfloat16) if a.dtype == jnp.float32 else a, x)


def layer_norm(values, norm_gain, norm_shift):
    center = values - jnp.mean(values, axis=-1, keepdims=True)
    factor = lax.rsqrt(jnp.mean(center * center, axis=-1, keepdims=True) + EPSILON)
    normed = center * factor
    return (normed * norm_gain + norm_shift, normed, factor)


def norm_back(gradient, normed, factor, norm_gain):
    scaled = gradient * norm_gain
    inner_term = (
        scaled
        - jnp.mean(scaled, axis=-1, keepdims=True)
        - normed * jnp.mean(scaled * normed, axis=-1, keepdims=True)
    )
    return inner_term * factor


def gelu_slope(values):
    normal_cdf = 0.5 * (1.0 + lax.erf(values * (1.0 / math.sqrt(2.0))))
    return normal_cdf + values * jnp.exp(-0.5 * values * values) * (1.0 / math.sqrt(2.0 * math.pi))


def scores_of(query_rows, key_rows, query_segment, key_segment, score_scale):
    raw_scores = jnp.einsum(
        "rqhd,rkhd->rhqk", query_rows, key_rows, preferred_element_type=jnp.float32
    )
    same_doc = (query_segment[:, :, None] == key_segment[:, None, :])[:, None]
    return jnp.where(same_doc, score_scale * raw_scores, NEGATIVE)


def contribute(
    query_rows,
    push_grad,
    delta_term,
    peak_term,
    query_segment,
    key_rows,
    value_rows,
    key_segment,
    score_scale,
):
    scores = scores_of(query_rows, key_rows, query_segment, key_segment, score_scale)
    weights = jnp.exp(scores - peak_term[..., None])
    pushed = jnp.einsum(
        "rqhd,rkhd->rhqk", push_grad, value_rows, preferred_element_type=jnp.float32
    )
    dscore = (weights * (pushed - delta_term[..., None]) * score_scale).astype(jnp.bfloat16)
    query_part = jnp.einsum("rhqk,rkhd->rqhd", dscore, key_rows, preferred_element_type=jnp.float32)
    key_part = jnp.einsum("rhqk,rqhd->rkhd", dscore, query_rows, preferred_element_type=jnp.float32)
    value_part = jnp.einsum(
        "rhqk,rqhd->rkhd",
        weights.astype(jnp.bfloat16),
        push_grad,
        preferred_element_type=jnp.float32,
    )
    return (query_part, key_part, value_part)


def body(
    hidden_in,
    segment_ids,
    queries,
    targets,
    cotangent,
    query_weight,
    key_weight,
    value_weight,
    output_weight,
    query_bias,
    value_bias,
    output_bias,
    first_gain,
    first_shift,
    inner_weight,
    inner_bias,
    outer_weight,
    outer_bias,
    second_gain,
    second_shift,
):
    shards = (
        query_weight,
        key_weight,
        value_weight,
        output_weight,
        query_bias,
        value_bias,
        output_bias,
        first_gain,
        first_shift,
        inner_weight,
        inner_bias,
        outer_weight,
        outer_bias,
        second_gain,
        second_shift,
    )
    cycle_size = lax.axis_size("blk")
    cycle_place = lax.axis_index("blk")
    micro_count, row_count, block_tokens, model_width = hidden_in.shape
    segment_count = queries.shape[1] // row_count
    head_count = HEADS
    head_dim = model_width // head_count
    score_scale = 1.0 / math.sqrt(head_dim)
    token_count = row_count * block_tokens
    head_shape = (row_count, block_tokens, head_count, head_dim)
    grad_totals = tuple((jnp.zeros(shard_piece.shape, jnp.float32) for shard_piece in shards))
    local_sum = None
    gathered = None
    out_list, embed_list, loss_list, qgrad_list, hgrad_list = ([], [], [], [], [])
    for micro_index in range(micro_count):
        gathered = (
            lax.all_gather(shards[0], "dp", axis=0, tiled=True),
            lax.all_gather(shards[1], "dp", axis=0, tiled=True),
            lax.all_gather(shards[2], "dp", axis=0, tiled=True),
            lax.all_gather(shards[3], "dp", axis=0, tiled=True),
            lax.all_gather(shards[4], "dp", axis=0, tiled=True),
            lax.all_gather(shards[5], "dp", axis=0, tiled=True),
            lax.all_gather(shards[6], "dp", axis=0, tiled=True),
            lax.all_gather(shards[7], "dp", axis=0, tiled=True),
            lax.all_gather(shards[8], "dp", axis=0, tiled=True),
            lax.all_gather(shards[9], "dp", axis=0, tiled=True),
            lax.all_gather(shards[10], "dp", axis=0, tiled=True),
            lax.all_gather(shards[11], "dp", axis=0, tiled=True),
            lax.all_gather(shards[12], "dp", axis=0, tiled=True),
            lax.all_gather(shards[13], "dp", axis=0, tiled=True),
            lax.all_gather(shards[14], "dp", axis=0, tiled=True),
        )
        (
            wq_full,
            wk_full,
            wv_full,
            wo_full,
            bq_full,
            bv_full,
            bo_full,
            gain_one,
            shift_one,
            w_inner,
            b_inner,
            w_outer,
            b_outer,
            gain_two,
            shift_two,
        ) = gathered
        gain_one = gain_one.astype(jnp.float32)
        gain_two = gain_two.astype(jnp.float32)
        segment = segment_ids[micro_index]
        flat_rows = hidden_in[micro_index].reshape(token_count, model_width)
        query_rows = (
            (
                jnp.dot(flat_rows, wq_full, preferred_element_type=jnp.float32)
                + bq_full.astype(jnp.float32)
            )
            .astype(jnp.bfloat16)
            .reshape(head_shape)
        )
        key_rows = (
            jnp.dot(flat_rows, wk_full, preferred_element_type=jnp.float32)
            .astype(jnp.bfloat16)
            .reshape(head_shape)
        )
        value_rows = (
            (
                jnp.dot(flat_rows, wv_full, preferred_element_type=jnp.float32)
                + bv_full.astype(jnp.float32)
            )
            .astype(jnp.bfloat16)
            .reshape(head_shape)
        )

        def absorb(softmax_state, visit_keys, visit_values, visit_segment):
            running_peak, running_total, running_sum = softmax_state
            scores = scores_of(query_rows, visit_keys, segment, visit_segment, score_scale)
            new_peak = jnp.maximum(running_peak, jnp.max(scores, axis=-1))
            decay_factor = jnp.exp(running_peak - new_peak)
            weights = jnp.exp(scores - new_peak[..., None])
            running_total = running_total * decay_factor + jnp.sum(weights, axis=-1)
            update = jnp.einsum(
                "rhqk,rkhd->rqhd",
                weights.astype(jnp.bfloat16),
                visit_values,
                preferred_element_type=jnp.float32,
            )
            running_sum = running_sum * jnp.transpose(decay_factor, (0, 2, 1))[..., None] + update
            return (new_peak, running_total, running_sum)

        start_state = (
            jnp.full((row_count, head_count, block_tokens), -1e30, jnp.float32),
            jnp.zeros((row_count, head_count, block_tokens), jnp.float32),
            jnp.zeros(head_shape, jnp.float32),
        )
        first_state = absorb(start_state, key_rows, value_rows, segment)

        def forward_step(cycle_step, cycle_carry):
            visit_keys, visit_values, visit_segment, prior_segment, softmax_state = cycle_carry
            visit_keys, visit_values, visit_segment = passed_along(
                (visit_keys, visit_values, visit_segment), "blk", 1
            )
            prior_segment = jnp.where(cycle_step == 1, visit_segment[:, -1], prior_segment)
            return (
                visit_keys,
                visit_values,
                visit_segment,
                prior_segment,
                absorb(softmax_state, visit_keys, visit_values, visit_segment),
            )

        cycle_carry = lax.fori_loop(
            1, cycle_size, forward_step, (key_rows, value_rows, segment, segment[:, 0], first_state)
        )
        prior_segment = cycle_carry[3]
        row_peak, row_total, running_sum = cycle_carry[4]
        total_heads = jnp.transpose(row_total, (0, 2, 1))[..., None]
        context = running_sum / total_heads
        context_low = context.reshape(token_count, model_width).astype(jnp.bfloat16)
        attended = jnp.dot(
            context_low, wo_full, preferred_element_type=jnp.float32
        ) + bo_full.astype(jnp.float32)
        first_out, first_normed, first_factor = layer_norm(
            flat_rows.astype(jnp.float32) + attended, gain_one, shift_one.astype(jnp.float32)
        )
        first_low = first_out.astype(jnp.bfloat16)
        inner_pre = jnp.dot(
            first_low, w_inner, preferred_element_type=jnp.float32
        ) + b_inner.astype(jnp.float32)
        active = jax.nn.gelu(inner_pre, approximate=False).astype(jnp.bfloat16)
        outer_out = jnp.dot(active, w_outer, preferred_element_type=jnp.float32) + b_outer.astype(
            jnp.float32
        )
        output, second_normed, second_factor = layer_norm(
            first_out + outer_out, gain_two, shift_two.astype(jnp.float32)
        )
        output_low = output.astype(jnp.bfloat16)
        out_list.append(output_low.reshape(row_count, block_tokens, model_width))
        position = cycle_place * block_tokens + jnp.arange(block_tokens, dtype=jnp.int32)
        before = jnp.concatenate([prior_segment[:, None], segment[:, :-1]], axis=1)
        leading = (position[None, :] == 0) | (segment != before)
        numbers = jnp.arange(segment_count, dtype=jnp.int32)
        select = (leading[:, None, :] & (segment[:, None, :] == numbers[None, :, None])).astype(
            jnp.float32
        )
        cls_table = jnp.einsum(
            "rsi,rid->rsd",
            select.astype(jnp.bfloat16),
            output_low.reshape(row_count, block_tokens, model_width),
            preferred_element_type=jnp.float32,
        )
        own_table = lax.psum(cls_table.astype(jnp.bfloat16), "blk").reshape(
            row_count * segment_count, model_width
        )
        embed_list.append(own_table)
        everyone = lax.all_gather(own_table, "dp", axis=0, tiled=True)
        query_vectors = queries[micro_index]
        query_scores = jnp.dot(query_vectors, everyone.T, preferred_element_type=jnp.float32)
        score_peak = jnp.max(query_scores, axis=1, keepdims=True)
        log_total = score_peak[:, 0] + jnp.log(jnp.sum(jnp.exp(query_scores - score_peak), axis=1))
        target_hot = (
            jnp.arange(query_scores.shape[1], dtype=jnp.int32)[None, :]
            == targets[micro_index][:, None]
        ).astype(jnp.float32)
        loss_list.append(log_total - jnp.sum(query_scores * target_hot, axis=1))
        dscore_query = jnp.exp(query_scores - log_total[:, None]) - target_hot
        qgrad_list.append(jnp.dot(dscore_query, everyone.astype(jnp.float32), precision=PRECISE))
        embed_part = jnp.dot(dscore_query.T, query_vectors.astype(jnp.float32), precision=PRECISE)
        embed_grad = (
            lax.psum_scatter(embed_part.astype(jnp.bfloat16), "dp", scatter_dimension=0, tiled=True)
            .astype(jnp.float32)
            .reshape(row_count, segment_count, model_width)
        )
        cls_grad = jnp.einsum("rsi,rsd->rid", select, embed_grad, precision=PRECISE)
        dout = cotangent[micro_index].reshape(token_count, model_width).astype(
            jnp.float32
        ) + cls_grad.reshape(token_count, model_width)
        gain_two_grad = jnp.sum(dout * second_normed, axis=0)
        shift_two_grad = jnp.sum(dout, axis=0)
        dsecond = norm_back(dout, second_normed, second_factor, gain_two)
        douter = dsecond.astype(jnp.bfloat16)
        outer_bias_grad = jnp.sum(douter.astype(jnp.float32), axis=0)
        outer_weight_grad = jnp.einsum(
            "nf,nd->fd", active, douter, preferred_element_type=jnp.float32
        )
        dactive = jnp.einsum("nd,fd->nf", douter, w_outer, preferred_element_type=jnp.float32)
        dinner = (dactive * gelu_slope(inner_pre)).astype(jnp.bfloat16)
        inner_bias_grad = jnp.sum(dinner.astype(jnp.float32), axis=0)
        inner_weight_grad = jnp.einsum(
            "nd,nf->df", first_low, dinner, preferred_element_type=jnp.float32
        )
        dfirst = dsecond + jnp.einsum(
            "nf,df->nd", dinner, w_inner, preferred_element_type=jnp.float32
        )
        gain_one_grad = jnp.sum(dfirst * first_normed, axis=0)
        shift_one_grad = jnp.sum(dfirst, axis=0)
        dresidual = norm_back(dfirst, first_normed, first_factor, gain_one)
        dattended = dresidual.astype(jnp.bfloat16)
        output_bias_grad = jnp.sum(dattended.astype(jnp.float32), axis=0)
        output_weight_grad = jnp.einsum(
            "nd,ne->de", context_low, dattended, preferred_element_type=jnp.float32
        )
        dcontext = jnp.einsum(
            "ne,de->nd", dattended, wo_full, preferred_element_type=jnp.float32
        ).astype(jnp.bfloat16)
        dcontext_wide = dcontext.astype(jnp.float32).reshape(head_shape)
        push_grad = (dcontext_wide / total_heads).astype(jnp.bfloat16)
        delta_term = jnp.transpose(
            jnp.sum(dcontext_wide * context, axis=-1) / total_heads[..., 0], (0, 2, 1)
        )
        own_query, own_key, own_value = contribute(
            query_rows,
            push_grad,
            delta_term,
            row_peak,
            segment,
            key_rows,
            value_rows,
            segment,
            score_scale,
        )

        def key_step(cycle_step, cycle_carry):
            visit_keys, visit_values, visit_segment, query_sum, key_sum, value_sum = cycle_carry
            visit_keys, visit_values, visit_segment = passed_along(
                (visit_keys, visit_values, visit_segment), "blk", 1
            )
            key_sum, value_sum = (
                passed_along(key_sum.astype(jnp.bfloat16), "blk", 1).astype(key_sum.dtype),
                passed_along(value_sum.astype(jnp.bfloat16), "blk", 1).astype(value_sum.dtype),
            )
            query_part, key_part, value_part = contribute(
                query_rows,
                push_grad,
                delta_term,
                row_peak,
                segment,
                visit_keys,
                visit_values,
                visit_segment,
                score_scale,
            )
            return (
                visit_keys,
                visit_values,
                visit_segment,
                query_sum + query_part,
                key_sum + key_part,
                value_sum + value_part,
            )

        back_carry = lax.fori_loop(
            1, cycle_size, key_step, (key_rows, value_rows, segment, own_query, own_key, own_value)
        )
        query_sum = back_carry[3]
        key_sum, value_sum = (
            passed_along(back_carry[4].astype(jnp.bfloat16), "blk", 1).astype(jnp.float32),
            passed_along(back_carry[5].astype(jnp.bfloat16), "blk", 1).astype(jnp.float32),
        )
        dquery = query_sum.astype(jnp.bfloat16).reshape(token_count, model_width)
        dkey = key_sum.astype(jnp.bfloat16).reshape(token_count, model_width)
        dvalue = value_sum.astype(jnp.bfloat16).reshape(token_count, model_width)
        dhidden = dresidual + jnp.einsum(
            "ne,de->nd", dquery, wq_full, preferred_element_type=jnp.float32
        )
        dhidden = dhidden + jnp.einsum(
            "ne,de->nd", dkey, wk_full, preferred_element_type=jnp.float32
        )
        dhidden = dhidden + jnp.einsum(
            "ne,de->nd", dvalue, wv_full, preferred_element_type=jnp.float32
        )
        hgrad_list.append(
            dhidden.astype(jnp.bfloat16).reshape(row_count, block_tokens, model_width)
        )
        local_grads = (
            jnp.einsum("nd,ne->de", flat_rows, dquery, preferred_element_type=jnp.float32),
            jnp.einsum("nd,ne->de", flat_rows, dkey, preferred_element_type=jnp.float32),
            jnp.einsum("nd,ne->de", flat_rows, dvalue, preferred_element_type=jnp.float32),
            output_weight_grad,
            jnp.sum(dquery.astype(jnp.float32), axis=0),
            jnp.sum(dvalue.astype(jnp.float32), axis=0),
            output_bias_grad,
            gain_one_grad,
            shift_one_grad,
            inner_weight_grad,
            inner_bias_grad,
            outer_weight_grad,
            outer_bias_grad,
            gain_two_grad,
            shift_two_grad,
        )
        local_sum = local_grads
        reduced = jax.tree.map(
            lambda part: part.astype(jnp.float32),
            lax.psum_scatter(as_sent(local_sum), "dp", scatter_dimension=0, tiled=True),
        )
        reduced = jax.tree.map(
            lambda part: part.astype(jnp.float32), lax.psum(as_sent(reduced), "blk")
        )
        grad_totals = tuple(
            (total_piece + new_piece for total_piece, new_piece in zip(grad_totals, reduced))
        )
        local_sum = None
    return (
        jnp.stack(out_list),
        jnp.stack(embed_list),
        jnp.stack(loss_list),
        jnp.stack(qgrad_list),
        jnp.stack(hgrad_list),
        grad_totals[0],
        grad_totals[1],
        grad_totals[2],
        grad_totals[3],
        grad_totals[4],
        grad_totals[5],
        grad_totals[6],
        grad_totals[7],
        grad_totals[8],
        grad_totals[9],
        grad_totals[10],
        grad_totals[11],
        grad_totals[12],
        grad_totals[13],
        grad_totals[14],
    )


def solution(mesh):
    in_specs = (
        P(None, "dp", "blk", None),
        P(None, "dp", "blk"),
        P(None, "dp", None),
        P(None, "dp"),
        P(None, "dp", "blk", None),
        P("dp", None),
        P("dp", None),
        P("dp", None),
        P("dp", None),
        P("dp"),
        P("dp"),
        P("dp"),
        P("dp"),
        P("dp"),
        P("dp", None),
        P("dp"),
        P("dp", None),
        P("dp"),
        P("dp"),
        P("dp"),
    )
    out_specs = (
        P(None, "dp", "blk", None),
        P(None, "dp", None),
        P(None, "dp"),
        P(None, "dp", None),
        P(None, "dp", "blk", None),
        P("dp", None),
        P("dp", None),
        P("dp", None),
        P("dp", None),
        P("dp"),
        P("dp"),
        P("dp"),
        P("dp"),
        P("dp"),
        P("dp", None),
        P("dp"),
        P("dp", None),
        P("dp"),
        P("dp"),
        P("dp"),
    )
    return jax.shard_map(body, mesh=mesh, in_specs=in_specs, out_specs=out_specs, check_vma=False)
```

profile of v0, /device:TPU:0, one launch (start us, length us, event | category | flops | bytes accessed | tf_op | source)
XLA Modules:
  0.0 1354.4 jit_solution(16652352997404749472)
XLA Ops:
  25.9 25.8 %all-reduce.27 = (bf16[768]{0:T(1024)(128)(2,1)S(1)}, bf16[768]{0:T(1024)(128)(2,1)S(1)}, bf16[768]{0:T(1024)(128)(2,1)S(1)}, bf16[768]{0:T(1024)(128)(2,1)S(1)}...) all-reduce(bf16[768]{0:T(1024)(128)(2,1)S(1)} %dynamic-update-slice, ...), channel_id=1, replica_groups=mesh['dp'=8,'blk'=4] {'dp'}, use_global_device_ids=true, to_apply=%add | all-reduce | flops 6144 | bytes 24576
  73.7 15.1 %all-gather.14.cloned.1.call-done = bf16[768,768]{1,0:T(8,128)(2,1)} async-done(((bf16[96,768]{1,0:T(8,128)(2,1)}), bf16[768,768]{1,0:T(8,128)(2,1)}) %all-gather.14.cloned.1.call-update) | async-done | bytes 1179664 | tf_op jit(solution)/shard_map/all_gather | solution.py:137
  110.1 71.5 %while.90 = (s32[]{:T(128)}, bf16[1,256,12,64]{1,3,2,0:T(8,128)(2,1)}, bf16[1,256,12,64]{1,3,2,0:T(8,128)(2,1)}, s32[1,256]{1,0:T(1,128)}, s32[1]{0:T(128)}, /*i...) while((s32[]{:T(128)}, ...), condition=%wide.region_5.6_spmd, body=%wide.region_2.5_spmd.sunk | while | flops 210445312 | bytes 17523032 | solution.py:233
  114.9 9.5 collective-permute-done.2
  137.1 11.4 collective-permute-done.2
  158.9 13.2 collective-permute-done.2
  181.7 58.7 %while.91 = (s32[]{:T(128)}, bf16[1,256,12,64]{1,3,2,0:T(8,128)(2,1)}, bf16[1,256,12,64]{1,3,2,0:T(8,128)(2,1)}, s32[1,256]{1,0:T(1,128)}, s32[1]{0:T(128)}, /*i...) while((s32[]{:T(128)}, ...), condition=%wide.region_15.16_spmd, body=%wide.region_12.0_spmd.sunk | while | flops 210445312 | bytes 17473852 | solution.py:233
  182.5 11.7 collective-permute-done.5
  250.5 11.9 fusion.105
  267.3 9.4 fusion.102
  281.7 17.2 %all-reduce.29 = (bf16[1,16,768]{2,1,0:T(8,128)(2,1)}, bf16[1,16,768]{2,1,0:T(8,128)(2,1)}) all-reduce(bf16[1,16,768]{2,1,0:T(8,128)(2,1)} %fusion.187, bf16[1,16,768]{2,1,0:T(8,128)(2,1)} %fusion.186), channel_id=1, replica_groups=mesh['dp'=8,'blk'=4] {'blk'}, use_global_device_ids=true, to_apply=%region_21.22 | all-reduce | flops 24576 | bytes 98304 | tf_op jit(solution)/shard_map/psum | solution.py:273
  298.9 9.2 all-gather.1
  328.4 27.5 %reduce-scatter.29.cloned.1.call-done = bf16[16,768]{1,0:T(8,128)(2,1)} async-done(((bf16[128,768]{1,0:T(8,128)(2,1)}), bf16[16,768]{1,0:T(8,128)(2,1)}) %reduce-scatter.29.cloned.1.call-update) | async-done | bytes 24592 | tf_op jit(solution)/shard_map/reduce_scatter | solution.py:291
  358.0 35.2 %reduce-scatter.27.cloned.1.call-done = bf16[16,768]{1,0:T(8,128)(2,1)} async-done(((bf16[128,768]{1,0:T(8,128)(2,1)}), bf16[16,768]{1,0:T(8,128)(2,1)}) %reduce-scatter.27.cloned.1.call-update) | async-done | bytes 24592 | tf_op jit(solution)/shard_map/reduce_scatter | solution.py:291
  443.4 119.2 %while.93 = (s32[]{:T(128)}, bf16[1,256,12,64]{1,3,2,0:T(8,128)(2,1)}, bf16[1,256,12,64]{1,3,2,0:T(8,128)(2,1)}, s32[1,256]{1,0:T(1,128)}, f32[1,256,12,64]{1,3,...) while((s32[]{:T(128)}, ...), condition=%wide.region_43.44_spmd, body=%wide.region_42.43_spmd.sunk | while | flops 513409024 | bytes 29782396 | solution.py:373
  568.5 108.1 %while.92 = (s32[]{:T(128)}, bf16[1,256,12,64]{1,3,2,0:T(8,128)(2,1)S(1)}, bf16[1,256,12,64]{1,3,2,0:T(8,128)(2,1)}, s32[1,256]{1,0:T(1,128)}, f32[1,256,12,64]{...) while((s32[]{:T(128)}, ...), condition=%wide.region_35.36_spmd, body=%wide.region_34.35_spmd.sunk | while | flops 513409024 | bytes 29782396 | solution.py:373
  681.2 10.3 collective-permute-done.18
  694.3 11.4 collective-permute-done.16
  708.6 12.5 collective-permute-done.19
  723.9 9.6 collective-permute-done.17
  783.6 12.1 reduce-scatter.47.cloned.1.call-done
  797.4 38.3 %reduce-scatter.53.cloned.1.call-done = bf16[96,768]{1,0:T(8,128)(2,1)} async-done(((bf16[768,768]{1,0:T(8,128)(2,1)}), bf16[96,768]{1,0:T(8,128)(2,1)}) %reduce-scatter.53.cloned.1.call-update) | async-done | bytes 147472
  837.4 38.5 %reduce-scatter.51.cloned.1.call-done = bf16[96,768]{1,0:T(8,128)(2,1)} async-done(((bf16[768,768]{1,0:T(8,128)(2,1)}), bf16[96,768]{1,0:T(8,128)(2,1)}) %reduce-scatter.51.cloned.1.call-update) | async-done | bytes 147472
  877.6 38.2 %reduce-scatter.33.cloned.1.call-done = bf16[96,768]{1,0:T(8,128)(2,1)} async-done(((bf16[768,768]{1,0:T(8,128)(2,1)}), bf16[96,768]{1,0:T(8,128)(2,1)}) %reduce-scatter.33.cloned.1.call-update) | async-done | bytes 147472 | tf_op jit(solution)/shard_map/reduce_scatter | solution.py:416
  915.8 40.2 %reduce-scatter.31.cloned.1.call-done = bf16[96,768]{1,0:T(8,128)(2,1)} async-done(((bf16[768,768]{1,0:T(8,128)(2,1)}), bf16[96,768]{1,0:T(8,128)(2,1)}) %reduce-scatter.31.cloned.1.call-update) | async-done | bytes 147472 | tf_op jit(solution)/shard_map/reduce_scatter | solution.py:416
  956.0 57.2 %reduce-scatter.37.cloned.1.call-done = bf16[96,3072]{1,0:T(8,128)(2,1)} async-done(((bf16[768,3072]{1,0:T(8,128)(2,1)}), bf16[96,3072]{1,0:T(8,128)(2,1)}) %reduce-scatter.37.cloned.1.call-update) | async-done | bytes 589840 | tf_op jit(solution)/shard_map/reduce_scatter | solution.py:416
  1013.2 57.6 %reduce-scatter.35.cloned.1.call-done = bf16[96,3072]{1,0:T(8,128)(2,1)} async-done(((bf16[768,3072]{1,0:T(8,128)(2,1)}), bf16[96,3072]{1,0:T(8,128)(2,1)}) %reduce-scatter.35.cloned.1.call-update) | async-done | bytes 589840 | tf_op jit(solution)/shard_map/reduce_scatter | solution.py:416
  1070.8 57.3 %reduce-scatter.41.cloned.1.call-done = bf16[384,768]{1,0:T(8,128)(2,1)} async-done(((bf16[3072,768]{1,0:T(8,128)(2,1)}), bf16[384,768]{1,0:T(8,128)(2,1)}) %reduce-scatter.41.cloned.1.call-update) | async-done | bytes 589840 | tf_op jit(solution)/shard_map/reduce_scatter | solution.py:416
  1128.2 57.6 %reduce-scatter.39.cloned.1.call-done = bf16[384,768]{1,0:T(8,128)(2,1)} async-done(((bf16[3072,768]{1,0:T(8,128)(2,1)}), bf16[384,768]{1,0:T(8,128)(2,1)}) %reduce-scatter.39.cloned.1.call-update) | async-done | bytes 589840 | tf_op jit(solution)/shard_map/reduce_scatter | solution.py:416
  1191.2 26.0 %all-reduce.26 = (bf16[768]{0:T(1024)(128)(2,1)}, bf16[768]{0:T(1024)(128)(2,1)}, bf16[768]{0:T(1024)(128)(2,1)}, bf16[768]{0:T(1024)(128)(2,1)}, bf16[768]{0:T(...) all-reduce(bf16[768]{0:T(1024)(128)(2,1)} %reduce_sum.487, ...), channel_id=15, replica_groups=mesh['dp'=8,'blk'=4] {'dp'}, use_global_device_ids=true, to_apply=%region_64.65.clone | all-reduce | flops 18432 | bytes 73728
  1238.0 21.5 %all-reduce.28 = (bf16[96]{0:T(256)(128)(2,1)}, bf16[96]{0:T(256)(128)(2,1)}, bf16[96]{0:T(256)(128)(2,1)}, bf16[96]{0:T(256)(128)(2,1)}, bf16[96]{0:T(256)(128)...) all-reduce(bf16[96]{0:T(256)(128)(2,1)} %dynamic-slice.11, ...), channel_id=1, replica_groups=mesh['dp'=8,'blk'=4] {'blk'}, use_global_device_ids=true, to_apply=%region_65.66 | all-reduce | flops 2304 | bytes 9216 | tf_op jit(solution)/shard_map/psum | solution.py:419
  1270.1 68.2 %all-reduce.33.cloned.1.call-done = (bf16[96,768]{0,1:T(8,128)(2,1)}, bf16[96,768]{0,1:T(8,128)(2,1)}, bf16[96,768]{0,1:T(8,128)(2,1)}, bf16[96,768]{0,1:T(8,128...) async-done(((bf16[96,768]{0,1:T(8,128)(2,1)}, ...) | async-done | bytes 3538960 | tf_op jit(solution)/shard_map/psum | solution.py:419
  (837 shorter events, 570.1 us)
Async XLA Ops:
  7.2 59.2 %all-gather.10.cloned.1.call-start = ((), (), s32[]{:S(2)}) async-start(), calls=%async_computation.14 | async-start | bytes 1327104 | tf_op jit(solution)/shard_map/all_gather | solution.py:138
  7.9 61.4 %all-gather.12.cloned.1.call-start = ((), (), s32[]{:S(2)}) async-start(), calls=%async_computation.15 | async-start | bytes 1327104 | tf_op jit(solution)/shard_map/all_gather | solution.py:139
  8.7 80.2 %all-gather.14.cloned.1.call-start = ((), (), s32[]{:S(2)}) async-start(), calls=%async_computation.16 | async-start | bytes 1327104 | tf_op jit(solution)/shard_map/all_gather | solution.py:137
  9.4 235.2 %all-gather.16.cloned.1.call-start = ((), (), s32[]{:S(2)}) async-start(), calls=%async_computation.17 | async-start | bytes 1327104 | tf_op jit(solution)/shard_map/all_gather | solution.py:140
  10.0 240.5 %all-gather.18.cloned.1.call-start = ((), (), s32[]{:S(2)}) async-start(), calls=%async_computation.18 | async-start | bytes 5308416 | tf_op jit(solution)/shard_map/all_gather | solution.py:146
  10.6 251.9 %all-gather.20.cloned.1.call-start = ((), (), s32[]{:S(2)}) async-start(), calls=%async_computation.19 | async-start | bytes 5308416 | tf_op jit(solution)/shard_map/all_gather | solution.py:148
  11.2 344.7 %reduce-scatter.29.cloned.1.call-start = ((), (), s32[]{:S(2)}) async-start(), calls=%async_computation.21 | async-start | bytes 221184 | tf_op jit(solution)/shard_map/reduce_scatter | solution.py:291
  323.6 69.7 %reduce-scatter.27.cloned.1.call-start = ((), (), s32[]{:S(2)}) async-start(), calls=%async_computation.20 | async-start | bytes 221184 | tf_op jit(solution)/shard_map/reduce_scatter | solution.py:291
  328.1 450.2 %reduce-scatter.45.cloned.1.call-start = ((), (), s32[]{:S(2)}) async-start(), calls=%async_computation.29 | async-start | bytes 1327104
  448.6 32.8 %collective-permute-start.15 = (bf16[1,256,12,64]{1,3,2,0:T(8,128)(2,1)}, bf16[1,256,12,64]{1,3,2,0:T(8,128)(2,1)}, u32[]{:S(2)}, u32[]{:S(2)}) collective-permute-start(bf16[1,256,12,64]{1,3,2,0:T(8,128)(2,1)} %get-tuple-element.1235), channel_id=1, source_target_pairs={{0,1},{1,2},{2,3},{3,0},{4,5},{5,6},{6,7},{7,4},{8,9},{9,10},{10,1... | collective-permute-start | bytes 1179656 | tf_op jit(solution)/shard_map/while/body/eval_jaxpr/ppermute | solution.py:18
  486.8 28.4 %collective-permute-start.14 = (bf16[1,256,12,64]{1,3,2,0:T(8,128)(2,1)}, bf16[1,256,12,64]{1,3,2,0:T(8,128)(2,1)}, u32[]{:S(2)}, u32[]{:S(2)}) collective-permute-start(bf16[1,256,12,64]{1,3,2,0:T(8,128)(2,1)} %get-tuple-element.1234), channel_id=1, source_target_pairs={{0,1},{1,2},{2,3},{3,0},{4,5},{5,6},{6,7},{7,4},{8,9},{9,10},{10,1... | collective-permute-start | bytes 1179656 | tf_op jit(solution)/shard_map/while/body/eval_jaxpr/ppermute | solution.py:18
  489.1 31.9 %collective-permute-start.15 = (bf16[1,256,12,64]{1,3,2,0:T(8,128)(2,1)}, bf16[1,256,12,64]{1,3,2,0:T(8,128)(2,1)}, u32[]{:S(2)}, u32[]{:S(2)}) collective-permute-start(bf16[1,256,12,64]{1,3,2,0:T(8,128)(2,1)} %get-tuple-element.1235), channel_id=1, source_target_pairs={{0,1},{1,2},{2,3},{3,0},{4,5},{5,6},{6,7},{7,4},{8,9},{9,10},{10,1... | collective-permute-start | bytes 1179656 | tf_op jit(solution)/shard_map/while/body/eval_jaxpr/ppermute | solution.py:18
  524.5 30.2 %collective-permute-start.14 = (bf16[1,256,12,64]{1,3,2,0:T(8,128)(2,1)}, bf16[1,256,12,64]{1,3,2,0:T(8,128)(2,1)}, u32[]{:S(2)}, u32[]{:S(2)}) collective-permute-start(bf16[1,256,12,64]{1,3,2,0:T(8,128)(2,1)} %get-tuple-element.1234), channel_id=1, source_target_pairs={{0,1},{1,2},{2,3},{3,0},{4,5},{5,6},{6,7},{7,4},{8,9},{9,10},{10,1... | collective-permute-start | bytes 1179656 | tf_op jit(solution)/shard_map/while/body/eval_jaxpr/ppermute | solution.py:18
  528.6 31.4 %collective-permute-start.15 = (bf16[1,256,12,64]{1,3,2,0:T(8,128)(2,1)}, bf16[1,256,12,64]{1,3,2,0:T(8,128)(2,1)}, u32[]{:S(2)}, u32[]{:S(2)}) collective-permute-start(bf16[1,256,12,64]{1,3,2,0:T(8,128)(2,1)} %get-tuple-element.1235), channel_id=1, source_target_pairs={{0,1},{1,2},{2,3},{3,0},{4,5},{5,6},{6,7},{7,4},{8,9},{9,10},{10,1... | collective-permute-start | bytes 1179656 | tf_op jit(solution)/shard_map/while/body/eval_jaxpr/ppermute | solution.py:18
  568.4 211.7 %reduce-scatter.43.cloned.1.call-start = ((), (), s32[]{:S(2)}) async-start(), calls=%async_computation.28 | async-start | bytes 1327104
  569.3 29.4 %collective-permute-start.9 = (bf16[1,256,12,64]{1,3,2,0:T(8,128)(2,1)}, bf16[1,256,12,64]{1,3,2,0:T(8,128)(2,1)S(1)}, u32[]{:S(2)}, u32[]{:S(2)}) collective-permute-start(bf16[1,256,12,64]{1,3,2,0:T(8,128)(2,1)} %get-tuple-element.1273), channel_id=1, source_target_pairs={{0,1},{1,2},{2,3},{3,0},{4,5},{5,6},{6,7},{7,4},{8,9},{9,10},{10,1... | collective-permute-start | bytes 1179656 | tf_op jit(solution)/shard_map/while/body/eval_jaxpr/ppermute | solution.py:18
  573.5 29.5 %collective-permute-start.10 = (bf16[1,256,12,64]{1,3,2,0:T(8,128)(2,1)}, bf16[1,256,12,64]{1,3,2,0:T(8,128)(2,1)}, u32[]{:S(2)}, u32[]{:S(2)}) collective-permute-start(bf16[1,256,12,64]{1,3,2,0:T(8,128)(2,1)} %get-tuple-element.1274), channel_id=1, source_target_pairs={{0,1},{1,2},{2,3},{3,0},{4,5},{5,6},{6,7},{7,4},{8,9},{9,10},{10,1... | collective-permute-start | bytes 1179656 | tf_op jit(solution)/shard_map/while/body/eval_jaxpr/ppermute | solution.py:18
  606.3 28.4 %collective-permute-start.9 = (bf16[1,256,12,64]{1,3,2,0:T(8,128)(2,1)}, bf16[1,256,12,64]{1,3,2,0:T(8,128)(2,1)S(1)}, u32[]{:S(2)}, u32[]{:S(2)}) collective-permute-start(bf16[1,256,12,64]{1,3,2,0:T(8,128)(2,1)} %get-tuple-element.1273), channel_id=1, source_target_pairs={{0,1},{1,2},{2,3},{3,0},{4,5},{5,6},{6,7},{7,4},{8,9},{9,10},{10,1... | collective-permute-start | bytes 1179656 | tf_op jit(solution)/shard_map/while/body/eval_jaxpr/ppermute | solution.py:18
  610.5 28.4 %collective-permute-start.10 = (bf16[1,256,12,64]{1,3,2,0:T(8,128)(2,1)}, bf16[1,256,12,64]{1,3,2,0:T(8,128)(2,1)}, u32[]{:S(2)}, u32[]{:S(2)}) collective-permute-start(bf16[1,256,12,64]{1,3,2,0:T(8,128)(2,1)} %get-tuple-element.1274), channel_id=1, source_target_pairs={{0,1},{1,2},{2,3},{3,0},{4,5},{5,6},{6,7},{7,4},{8,9},{9,10},{10,1... | collective-permute-start | bytes 1179656 | tf_op jit(solution)/shard_map/while/body/eval_jaxpr/ppermute | solution.py:18
  642.3 27.4 %collective-permute-start.9 = (bf16[1,256,12,64]{1,3,2,0:T(8,128)(2,1)}, bf16[1,256,12,64]{1,3,2,0:T(8,128)(2,1)S(1)}, u32[]{:S(2)}, u32[]{:S(2)}) collective-permute-start(bf16[1,256,12,64]{1,3,2,0:T(8,128)(2,1)} %get-tuple-element.1273), channel_id=1, source_target_pairs={{0,1},{1,2},{2,3},{3,0},{4,5},{5,6},{6,7},{7,4},{8,9},{9,10},{10,1... | collective-permute-start | bytes 1179656 | tf_op jit(solution)/shard_map/while/body/eval_jaxpr/ppermute | solution.py:18
  646.5 27.4 %collective-permute-start.10 = (bf16[1,256,12,64]{1,3,2,0:T(8,128)(2,1)}, bf16[1,256,12,64]{1,3,2,0:T(8,128)(2,1)}, u32[]{:S(2)}, u32[]{:S(2)}) collective-permute-start(bf16[1,256,12,64]{1,3,2,0:T(8,128)(2,1)} %get-tuple-element.1274), channel_id=1, source_target_pairs={{0,1},{1,2},{2,3},{3,0},{4,5},{5,6},{6,7},{7,4},{8,9},{9,10},{10,1... | collective-permute-start | bytes 1179656 | tf_op jit(solution)/shard_map/while/body/eval_jaxpr/ppermute | solution.py:18
  681.1 100.8 %reduce-scatter.49.cloned.1.call-start = ((), (), s32[]{:S(2)}) async-start(), calls=%async_computation.31 | async-start | bytes 1327104
  694.2 101.4 %reduce-scatter.47.cloned.1.call-start = ((), (), s32[]{:S(2)}) async-start(), calls=%async_computation.30 | async-start | bytes 1327104
  708.5 127.2 %reduce-scatter.53.cloned.1.call-start = ((), (), s32[]{:S(2)}) async-start(), calls=%async_computation.33 | async-start | bytes 1327104
  723.8 152.1 %reduce-scatter.51.cloned.1.call-start = ((), (), s32[]{:S(2)}) async-start(), calls=%async_computation.32 | async-start | bytes 1327104
  737.5 178.2 %reduce-scatter.33.cloned.1.call-start = ((), (), s32[]{:S(2)}) async-start(), calls=%async_computation.23 | async-start | bytes 1327104 | tf_op jit(solution)/shard_map/reduce_scatter | solution.py:416
  739.1 216.9 %reduce-scatter.31.cloned.1.call-start = ((), (), s32[]{:S(2)}) async-start(), calls=%async_computation.22 | async-start | bytes 1327104 | tf_op jit(solution)/shard_map/reduce_scatter | solution.py:416
  741.1 272.1 %reduce-scatter.37.cloned.1.call-start = ((), (), s32[]{:S(2)}) async-start(), calls=%async_computation.25 | async-start | bytes 5308416 | tf_op jit(solution)/shard_map/reduce_scatter | solution.py:416
  746.4 324.4 %reduce-scatter.35.cloned.1.call-start = ((), (), s32[]{:S(2)}) async-start(), calls=%async_computation.24 | async-start | bytes 5308416 | tf_op jit(solution)/shard_map/reduce_scatter | solution.py:416
  752.8 375.4 %reduce-scatter.41.cloned.1.call-start = ((), (), s32[]{:S(2)}) async-start(), calls=%async_computation.27 | async-start | bytes 5308416 | tf_op jit(solution)/shard_map/reduce_scatter | solution.py:416
  759.0 426.8 %reduce-scatter.39.cloned.1.call-start = ((), (), s32[]{:S(2)}) async-start(), calls=%async_computation.26 | async-start | bytes 5308416 | tf_op jit(solution)/shard_map/reduce_scatter | solution.py:416
  765.1 573.3 %all-reduce.33.cloned.1.call-start = ((), (), s32[]{:S(2)}) async-start(), calls=%async_computation.34 | async-start | bytes 7667712 | tf_op jit(solution)/shard_map/psum | solution.py:419
  (222 other events, 2594.7 us)
Sparse Core Ops, SparseCore 0:
  9.9 26.8 all-gather.9
  38.7 24.1 all-gather.11
  64.8 24.0 all-gather.13
  90.6 24.0 all-gather.15
  116.4 38.9 all-gather.17
  157.1 38.9 all-gather.19
  323.7 32.0 reduce-scatter.28
  359.7 33.4 reduce-scatter.26
  568.5 34.0 reduce-scatter.44
  681.2 34.1 reduce-scatter.42
  718.6 36.7 reduce-scatter.48
  758.8 36.7 reduce-scatter.46
  798.9 36.7 reduce-scatter.52
  839.1 36.7 reduce-scatter.50
  879.0 36.7 reduce-scatter.32
  919.2 36.7 reduce-scatter.30
  959.3 53.8 reduce-scatter.36
  1016.9 53.8 reduce-scatter.34
  1074.3 53.8 reduce-scatter.40
  1131.9 53.8 reduce-scatter.38
  1190.4 147.9 all-reduce.32
where the time goes:
time: 1370 us; the launch traced here: 1350 us
  waiting for transfers between devices  783 us (57%)
  matrix products  185 us (14%)
  local copies, waits for them, and re-layouts  137 us (10%)
  blocking collectives  116 us (8%)
  other arithmetic  59.6 us (4%)
  starting transfers between devices  43.5 us (3%)
  between operations  18.3 us (1%)
    reduce_scatter x6, waiting for transfers between devices, body(): lax.psum_scatter(as_sent(local_sum), 'dp', scatter_dimension=0, tiled=True)  308 us
    ppermute x52, waiting for transfers between devices, passed_along(): return lax.ppermute(x, axis, [(i, (i + by) % size) for i in range(size)])  236 us
    unnamed x27, waiting for transfers between devices  92.8 us
    unnamed x365, local copies, waits for them, and re-layouts  75.2 us
    psum x1, waiting for transfers between devices, body(): lax.psum(as_sent(reduced), 'blk')  68.2 us
    reduce_scatter x2, waiting for transfers between devices, body(): lax.psum_scatter(embed_part.astype(jnp.bfloat16), 'dp', scatter_dimension...  62.7 us
    unnamed x2, blocking collectives  51.8 us
    ppermute x52, starting transfers between devices, passed_along(): return lax.ppermute(x, axis, [(i, (i + by) % size) for i in range(size)])  42.1 us
  transfers between devices with their start and end apart: 73, of which 47 were waited for; matrix products, arithmetic and copies ran while one was open for 20% of the time, Pallas kernels for 0%

commit v1 on v0

--- a/solution.py
+++ b/solution.py
@@ -1,8 +1,11 @@
+import functools
 import math
 
 import jax
 import jax.numpy as jnp
 from jax import lax
+from jax.experimental import pallas as pl
+from jax.experimental.pallas import tpu as pltpu
 from jax.sharding import PartitionSpec as P
 
 HEADS = 12
@@ -80,7 +83,7 @@
     return (query_part, key_part, value_part)
 
 
-def body(
+def ring_body(
     hidden_in,
     segment_ids,
     queries,
@@ -446,6 +449,847 @@
     )
 
 
+MESH = pl.DeviceIdType.MESH
+VMEM_LIMIT = 60 * 1024 * 1024
+SIDE = {"c": 1, "x": 2, "y": 4}
+
+
+def place():
+    dp, blk = lax.axis_index("dp"), lax.axis_index("blk")
+    bits = {"c": lax.rem(dp, 2), "x": lax.rem(dp // 2, 2), "y": dp // 4}
+    return dp, blk, bits
+
+
+def across(dp, blk, bits, *axes):
+    other = dp
+    for axis in axes:
+        other = other + SIDE[axis] * (1 - 2 * bits[axis])
+    return (other, blk)
+
+
+def greet(peers):
+    barrier = pltpu.get_barrier_semaphore()
+    for peer in peers:
+        pl.semaphore_signal(barrier, inc=1, device_id=peer, device_id_type=MESH)
+    pl.semaphore_wait(barrier, len(peers))
+
+
+def remote(source, target, send_sem, recv_sem, peer):
+    return pltpu.make_async_remote_copy(
+        src_ref=source,
+        dst_ref=target,
+        send_sem=send_sem,
+        recv_sem=recv_sem,
+        device_id=peer,
+        device_id_type=MESH,
+    )
+
+
+def comm_params(collective):
+    return pltpu.CompilerParams(
+        collective_id=collective, has_side_effects=True, vmem_limit_bytes=VMEM_LIMIT
+    )
+
+
+ANY = pl.BlockSpec(memory_space=pl.ANY)
+IN_VMEM = pl.BlockSpec(memory_space=pltpu.VMEM)
+
+
+def gather_kernel(routes, ring_size, *refs):
+    count = len(routes)
+    shards, seg_shard = refs[:count], refs[count]
+    fulls, seg_full = refs[count + 1 : 2 * count + 1], refs[2 * count + 1]
+    send_sem, recv_sem, seg_send, seg_recv, local_sem = refs[2 * count + 2 :]
+    dp, blk, bits = place()
+    sibling = across(dp, blk, bits, "c")
+    ring = [(dp, lax.rem(blk + step, ring_size)) for step in range(1, ring_size)]
+    greet([sibling, across(dp, blk, bits, "x"), across(dp, blk, bits, "y")] + ring)
+    seg_rows = seg_shard.shape[0]
+    started = []
+    locals_started = []
+    for step, peer in enumerate(ring):
+        copy = remote(
+            seg_shard,
+            seg_full.at[pl.ds(blk * seg_rows, seg_rows)],
+            seg_send.at[step],
+            seg_recv.at[step],
+            peer,
+        )
+        copy.start()
+        started.append(copy)
+    copy = pltpu.make_async_copy(
+        seg_shard, seg_full.at[pl.ds(blk * seg_rows, seg_rows)], local_sem.at[count]
+    )
+    copy.start()
+    locals_started.append(copy)
+
+    def block(item, owner):
+        rows = shards[item].shape[0]
+        return fulls[item].at[pl.ds(owner * rows, rows)]
+
+    inbound = {}
+    for item, (first, second) in enumerate(routes):
+        for slot, peer in enumerate(
+            (across(dp, blk, bits, first), across(dp, blk, bits, second), sibling)
+        ):
+            copy = remote(
+                shards[item],
+                block(item, dp),
+                send_sem.at[item, slot],
+                recv_sem.at[item, slot],
+                peer,
+            )
+            copy.start()
+            inbound[item, slot] = copy
+        copy = pltpu.make_async_copy(shards[item], block(item, dp), local_sem.at[item])
+        copy.start()
+        locals_started.append(copy)
+    for item, (first, second) in enumerate(routes):
+        inbound[item, 0].wait_recv()
+        held = block(item, across(dp, blk, bits, first)[0])
+        for slot, peer in ((3, across(dp, blk, bits, second)), (4, sibling)):
+            copy = remote(held, held, send_sem.at[item, slot], recv_sem.at[item, slot], peer)
+            copy.start()
+            inbound[item, slot] = copy
+    for item, (first, second) in enumerate(routes):
+        inbound[item, 1].wait_recv()
+        held = block(item, across(dp, blk, bits, second)[0])
+        copy = remote(held, held, send_sem.at[item, 5], recv_sem.at[item, 5], sibling)
+        copy.start()
+        inbound[item, 5] = copy
+    for item, (first, second) in enumerate(routes):
+        inbound[item, 3].wait_recv()
+        held = block(item, across(dp, blk, bits, first, second)[0])
+        copy = remote(held, held, send_sem.at[item, 6], recv_sem.at[item, 6], sibling)
+        copy.start()
+        inbound[item, 6] = copy
+    for item in range(count):
+        for slot in (2, 4, 5, 6):
+            inbound[item, slot].wait_recv()
+        for slot in range(7):
+            inbound[item, slot].wait_send()
+    for copy in started:
+        copy.wait()
+    for copy in locals_started:
+        copy.wait()
+
+
+def gather_all(shards, routes, segments, dp_size, ring_size):
+    count = len(shards)
+    return pl.pallas_call(
+        functools.partial(gather_kernel, routes, ring_size),
+        out_shape=tuple(
+            jax.ShapeDtypeStruct((dp_size * s.shape[0], s.shape[1]), s.dtype) for s in shards
+        )
+        + (
+            jax.ShapeDtypeStruct((ring_size * segments.shape[0], segments.shape[1]), jnp.int32),
+        ),
+        in_specs=[ANY] * (count + 1),
+        out_specs=(ANY,) * (count + 1),
+        scratch_shapes=[
+            pltpu.SemaphoreType.DMA((count, 7)),
+            pltpu.SemaphoreType.DMA((count, 7)),
+            pltpu.SemaphoreType.DMA((ring_size,)),
+            pltpu.SemaphoreType.DMA((ring_size,)),
+            pltpu.SemaphoreType.DMA((count + 1,)),
+        ],
+        compiler_params=comm_params(1),
+    )(*shards, segments)
+
+
+def to_heads_kernel(ring_size, *refs):
+    count = (len(refs) - 4) // 1
+    parts, (out, send_sem, recv_sem, local_sem) = refs[:count], refs[count:]
+    dp, blk, _ = place()
+    greet([(dp, lax.rem(blk + step, ring_size)) for step in range(1, ring_size)])
+    micro, rows, tokens = parts[0].shape
+    group = rows // ring_size
+    copies = []
+    for m in range(micro):
+        for index, part in enumerate(parts):
+            for step in range(ring_size):
+                owner = lax.rem(blk + step, ring_size)
+                source = part.at[m, pl.ds(owner * group, group)]
+                target = out.at[m, index, :, pl.ds(pl.multiple_of(blk * tokens, tokens), tokens)]
+                if step == 0:
+                    copy = pltpu.make_async_copy(source, target, local_sem.at[m, index])
+                else:
+                    copy = remote(
+                        source,
+                        target,
+                        send_sem.at[m, index, step],
+                        recv_sem.at[m, index, step],
+                        (dp, owner),
+                    )
+                copy.start()
+                copies.append(copy)
+    for copy in copies:
+        copy.wait()
+
+
+def to_heads(parts, ring_size, collective):
+    micro, rows, tokens = parts[0].shape
+    count = len(parts)
+    return pl.pallas_call(
+        functools.partial(to_heads_kernel, ring_size),
+        out_shape=jax.ShapeDtypeStruct(
+            (micro, count, rows // ring_size, tokens * ring_size), parts[0].dtype
+        ),
+        in_specs=[ANY] * count,
+        out_specs=ANY,
+        scratch_shapes=[
+            pltpu.SemaphoreType.DMA((micro, count, ring_size)),
+            pltpu.SemaphoreType.DMA((micro, count, ring_size)),
+            pltpu.SemaphoreType.DMA((micro, count)),
+        ],
+        compiler_params=comm_params(collective),
+    )(*parts)
+
+
+def to_tokens_kernel(ring_size, *refs):
+    count = (len(refs) - 3) // 2
+    parts, outs = refs[:count], refs[count : 2 * count]
+    send_sem, recv_sem, local_sem = refs[2 * count :]
+    dp, blk, _ = place()
+    greet([(dp, lax.rem(blk + step, ring_size)) for step in range(1, ring_size)])
+    micro, group, length = parts[0].shape
+    tokens = length // ring_size
+    copies = []
+    for m in range(micro):
+        for index, (part, out) in enumerate(zip(parts, outs)):
+            for step in range(ring_size):
+                owner = lax.rem(blk + step, ring_size)
+                source = part.at[m, :, pl.ds(pl.multiple_of(owner * tokens, tokens), tokens)]
+                target = out.at[m, pl.ds(blk * group, group)]
+                if step == 0:
+                    copy = pltpu.make_async_copy(source, target, local_sem.at[m, index])
+                else:
+                    copy = remote(
+                        source,
+                        target,
+                        send_sem.at[m, index, step],
+                        recv_sem.at[m, index, step],
+                        (dp, owner),
+                    )
+                copy.start()
+                copies.append(copy)
+    for copy in copies:
+        copy.wait()
+
+
+def to_tokens(parts, ring_size, collective):
+    micro, group, length = parts[0].shape
+    count = len(parts)
+    out = pl.pallas_call(
+        functools.partial(to_tokens_kernel, ring_size),
+        out_shape=tuple(
+            jax.ShapeDtypeStruct((micro, group * ring_size, length // ring_size), p.dtype)
+            for p in parts
+        ),
+        in_specs=[ANY] * count,
+        out_specs=(ANY,) * count,
+        scratch_shapes=[
+            pltpu.SemaphoreType.DMA((micro, count, ring_size)),
+            pltpu.SemaphoreType.DMA((micro, count, ring_size)),
+            pltpu.SemaphoreType.DMA((micro, count)),
+        ],
+        compiler_params=comm_params(collective),
+    )(*parts)
+    return out
+
+
+def tables_kernel(ring_size, dp_size, own, out, arrived, send_sem, recv_sem, ring_send, ring_recv):
+    dp, blk, _ = place()
+    ring = [(dp, lax.rem(blk + step, ring_size)) for step in range(1, ring_size)]
+    group = [(lax.rem(dp + step, dp_size), blk) for step in range(1, dp_size)]
+    greet(ring + group)
+    copies = []
+    for step, peer in enumerate(ring):
+        copy = remote(own, arrived.at[step], ring_send.at[step], ring_recv.at[step], peer)
+        copy.start()
+        copies.append(copy)
+    for copy in copies:
+        copy.wait()
+    total = own[...].astype(jnp.float32)
+    for step in range(ring_size - 1):
+        total = total + arrived[step].astype(jnp.float32)
+    out[dp] = total.astype(out.dtype)
+    copies = []
+    for step, peer in enumerate(group):
+        copy = remote(out.at[dp], out.at[dp], send_sem.at[step], recv_sem.at[step], peer)
+        copy.start()
+        copies.append(copy)
+    for copy in copies:
+        copy.wait()
+
+
+def gather_tables(own, ring_size, dp_size):
+    return pl.pallas_call(
+        functools.partial(tables_kernel, ring_size, dp_size),
+        out_shape=jax.ShapeDtypeStruct((dp_size,) + own.shape, own.dtype),
+        in_specs=[IN_VMEM],
+        out_specs=IN_VMEM,
+        scratch_shapes=[
+            pltpu.VMEM((ring_size - 1,) + own.shape, own.dtype),
+            pltpu.SemaphoreType.DMA((dp_size,)),
+            pltpu.SemaphoreType.DMA((dp_size,)),
+            pltpu.SemaphoreType.DMA((ring_size,)),
+            pltpu.SemaphoreType.DMA((ring_size,)),
+        ],
+        compiler_params=comm_params(4),
+    )(own)
+
+
+def reduce_kernel(routes, *refs):
+    count = len(routes)
+    grads, outs = refs[:count], refs[count : 2 * count]
+    buffers = refs[2 * count : 2 * count + 7 * count]
+    own = buffers[:count]
+    from_core = buffers[count : 2 * count]
+    from_first = buffers[2 * count : 3 * count]
+    from_second = buffers[3 * count : 4 * count]
+    ring_one = buffers[4 * count : 5 * count]
+    ring_two = buffers[5 * count : 6 * count]
+    ring_three = buffers[6 * count : 7 * count]
+    send_sem, recv_sem, local_sem = refs[9 * count :]
+    dp, blk, bits = place()
+    sibling = across(dp, blk, bits, "c")
+    is_end = (blk == 0) | (blk == 3)
+    is_middle = (blk == 1) | (blk == 2)
+    partner = (dp, blk + 1 - 2 * lax.rem(blk, 2))
+    facing = (dp, 3 - blk)
+    greet(
+        [
+            sibling,
+            across(dp, blk, bits, "x"),
+            across(dp, blk, bits, "y"),
+            partner,
+            facing,
+        ]
+    )
+    sent = []
+
+    def owner(core, axes, first_bit, second_bit):
+        return core + SIDE[axes[0]] * first_bit + SIDE[axes[1]] * second_bit
+
+    def block(item, which):
+        rows = grads[item].shape[0] // 8
+        return grads[item].at[pl.ds(which * rows, rows)]
+
+    def go(source, target, item, slot, peer):
+        copy = remote(source, target, send_sem.at[item, slot], recv_sem.at[item, slot], peer)
+        copy.start()
+        return copy
+
+    flying = {}
+
+    def start_core(item):
+        axes = routes[item]
+        for f in range(2):
+            for s in range(2):
+                copy = go(
+                    block(item, owner(1 - bits["c"], axes, f, s)),
+                    from_core[item].at[f, s],
+                    item,
+                    2 * f + s,
+                    sibling,
+                )
+                flying[item, 2 * f + s] = copy
+                mine = pltpu.make_async_copy(
+                    block(item, owner(bits["c"], axes, f, s)),
+                    own[item].at[f, s],
+                    local_sem.at[item, 2 * f + s],
+                )
+                mine.start()
+                flying[item, "own", 2 * f + s] = mine
+
+    def added(left, right):
+        return (left.astype(jnp.float32) + right.astype(jnp.float32)).astype(jnp.bfloat16)
+
+    def after_core(item):
+        axes = routes[item]
+        mine = bits[axes[0]]
+        for slot in range(4):
+            flying[item, slot].wait_recv()
+            flying[item, "own", slot].wait()
+        for f in (1 - mine, mine):
+            for s in range(2):
+                own[item][f, s] = added(own[item][f, s], from_core[item][f, s])
+                if f is not mine:
+                    flying[item, 4 + s] = go(
+                        own[item].at[f, s],
+                        from_first[item].at[s],
+                        item,
+                        4 + s,
+                        across(dp, blk, bits, axes[0]),
+                    )
+
+    def after_first(item):
+        axes = routes[item]
+        f, mine = bits[axes[0]], bits[axes[1]]
+        for s in range(2):
+            flying[item, 4 + s].wait_recv()
+        own[item][f, 1 - mine] = added(own[item][f, 1 - mine], from_first[item][1 - mine])
+        flying[item, 6] = go(
+            own[item].at[f, 1 - mine],
+            from_second[item],
+            item,
+            6,
+            across(dp, blk, bits, axes[1]),
+        )
+        own[item][f, mine] = added(own[item][f, mine], from_first[item][mine])
+
+    def after_second(item):
+        axes = routes[item]
+        f, s = bits[axes[0]], bits[axes[1]]
+        flying[item, 6].wait_recv()
+        ring_one[item][0] = added(own[item][f, s], from_second[item][...])
+
+        def ring_copy(source, target, slot, peer):
+            return remote(source, target, send_sem.at[item, slot], recv_sem.at[item, slot], peer)
+
+        flying[item, 7] = ring_copy(ring_one[item].at[0], ring_one[item].at[1], 7, partner)
+        flying[item, 8] = ring_copy(ring_two[item].at[0], ring_two[item].at[1], 8, facing)
+        flying[item, 9] = ring_copy(ring_three[item].at[0], ring_three[item].at[1], 9, partner)
+
+        @pl.when(is_end)
+        def _():
+            flying[item, 7].start()
+
+    def at_middle(item):
+        @pl.when(is_middle)
+        def _():
+            flying[item, 7].wait_recv()
+            ring_two[item][0] = added(ring_one[item][0], ring_one[item][1])
+            flying[item, 8].start()
+
+    def across_middle(item):
+        @pl.when(is_middle)
+        def _():
+            flying[item, 8].wait_recv()
+            ring_three[item][0] = added(ring_two[item][0], ring_two[item][1])
+            flying[item, 9].start()
+            outs[item][...] = ring_three[item][0].astype(jnp.float32)
+
+    def at_end(item):
+        @pl.when(is_end)
+        def _():
+            flying[item, 9].wait_recv()
+            outs[item][...] = ring_three[item][1].astype(jnp.float32)
+
+    stages = (after_core, after_first, after_second, at_middle, across_middle, at_end)
+    for item in range(count):
+        start_core(item)
+    for tick in range(count + len(stages) - 1):
+        for depth in reversed(range(len(stages))):
+            item = tick - depth
+            if 0 <= item < count:
+                stages[depth](item)
+    for item in range(count):
+        for slot in range(7):
+            flying[item, slot].wait_send()
+
+    @pl.when(is_end)
+    def _():
+        for item in range(count):
+            flying[item, 7].wait_send()
+
+    @pl.when(is_middle)
+    def _():
+        for item in range(count):
+            flying[item, 8].wait_send()
+            flying[item, 9].wait_send()
+
+
+def reduce_all(grads, routes, collective):
+    count = len(grads)
+    shards = [(g.shape[0] // 8, g.shape[1]) for g in grads]
+    scratch = []
+    for lead in ((2, 2), (2, 2), (2,), (), (2,), (2,), (2,)):
+        scratch += [pltpu.VMEM(lead + shard, jnp.bfloat16) for shard in shards]
+    return pl.pallas_call(
+        functools.partial(reduce_kernel, routes),
+        out_shape=tuple(jax.ShapeDtypeStruct(shard, jnp.float32) for shard in shards),
+        in_specs=[ANY] * count,
+        out_specs=(IN_VMEM,) * count,
+        scratch_shapes=scratch
+        + [
+            pltpu.SemaphoreType.DMA((count, 10)),
+            pltpu.SemaphoreType.DMA((count, 10)),
+            pltpu.SemaphoreType.DMA((count, 4)),
+        ],
+        compiler_params=comm_params(collective),
+    )(*grads)
+
+
+def contract(left, right, left_dim, right_dim):
+    return lax.dot_general(
+        left, right, (((left_dim,), (right_dim,)), ((), ())), preferred_element_type=jnp.float32
+    )
+
+
+def attend_kernel(score_scale, block, qkv, seg_col, seg_row, context, low, stats):
+    queries_t, keys_t, values_t = qkv[0, 0, 0], qkv[0, 1, 0], qkv[0, 2, 0]
+    length = keys_t.shape[1]
+    keys = keys_t.T
+    for start in range(0, length, block):
+        span = slice(start, start + block)
+        raw = contract(keys, queries_t[:, span], 1, 0)
+        same = seg_col[0] == seg_row[0, :, span]
+        scores = jnp.where(same, raw * score_scale, NEGATIVE)
+        peak = jnp.max(scores, axis=0, keepdims=True)
+        weights = jnp.exp(scores - peak)
+        total = jnp.sum(weights, axis=0, keepdims=True)
+        gathered = contract(values_t, weights.astype(jnp.bfloat16), 1, 0)
+        ctx = gathered / total
+        context[0, 0, :, span] = ctx
+        low[0, 0, :, span] = ctx.astype(jnp.bfloat16)
+        stats[0, 0, 0:1, span] = peak
+        stats[0, 0, 1:2, span] = total
+
+
+def attend(qkv, seg_col, seg_row, score_scale):
+    micro, _, heads, depth, length = qkv.shape
+    block = min(256, length)
+    return pl.pallas_call(
+        functools.partial(attend_kernel, score_scale, block),
+        grid=(micro, heads),
+        out_shape=(
+            jax.ShapeDtypeStruct((micro, heads, depth, length), jnp.float32),
+            jax.ShapeDtypeStruct((micro, heads, depth, length), jnp.bfloat16),
+            jax.ShapeDtypeStruct((micro, heads, 2, length), jnp.float32),
+        ),
+        in_specs=[
+            pl.BlockSpec((1, 3, 1, depth, length), lambda m, h: (m, 0, h, 0, 0)),
+            pl.BlockSpec((1, length, 1), lambda m, h: (m, 0, 0)),
+            pl.BlockSpec((1, 1, length), lambda m, h: (m, 0, 0)),
+        ],
+        out_specs=(
+            pl.BlockSpec((1, 1, depth, length), lambda m, h: (m, h, 0, 0)),
+            pl.BlockSpec((1, 1, depth, length), lambda m, h: (m, h, 0, 0)),
+            pl.BlockSpec((1, 1, 2, length), lambda m, h: (m, h, 0, 0)),
+        ),
+        compiler_params=pltpu.CompilerParams(vmem_limit_bytes=VMEM_LIMIT),
+    )(qkv, seg_col, seg_row)
+
+
+def attend_back_kernel(
+    score_scale, block, qkv, seg_col, seg_row, context, stats, dcontext, dqueries, dkeys, dvalues
+):
+    queries_t, keys_t, values_t = qkv[0, 0, 0], qkv[0, 1, 0], qkv[0, 2, 0]
+    depth, length = keys_t.shape
+    keys, values = keys_t.T, values_t.T
+    dkey_sum = jnp.zeros((depth, length), jnp.float32)
+    dvalue_sum = jnp.zeros((depth, length), jnp.float32)
+    for start in range(0, length, block):
+        span = slice(start, start + block)
+        peak, total = stats[0, 0, 0:1, span], stats[0, 0, 1:2, span]
+        dctx = dcontext[0, 0, :, span].astype(jnp.float32)
+        push = (dctx / total).astype(jnp.bfloat16)
+        delta = jnp.sum(dctx * context[0, 0, :, span], axis=0, keepdims=True) / total
+        raw = contract(keys, queries_t[:, span], 1, 0)
+        same = seg_col[0] == seg_row[0, :, span]
+        weights = jnp.exp(jnp.where(same, raw * score_scale, NEGATIVE) - peak)
+        pushed = contract(values, push, 1, 0)
+        dscore = (weights * (pushed - delta) * score_scale).astype(jnp.bfloat16)
+        dqueries[0, 0, :, span] = contract(keys_t, dscore, 1, 0).astype(jnp.bfloat16)
+        dkey_sum = dkey_sum + contract(queries_t[:, span], dscore, 1, 1)
+        dvalue_sum = dvalue_sum + contract(push, weights.astype(jnp.bfloat16), 1, 1)
+    dkeys[0, 0] = dkey_sum.astype(jnp.bfloat16)
+    dvalues[0, 0] = dvalue_sum.astype(jnp.bfloat16)
+
+
+def attend_back(qkv, seg_col, seg_row, context, stats, dcontext, score_scale):
+    micro, _, heads, depth, length = qkv.shape
+    block = min(256, length)
+    head_block = pl.BlockSpec((1, 1, depth, length), lambda m, h: (m, h, 0, 0))
+    return pl.pallas_call(
+        functools.partial(attend_back_kernel, score_scale, block),
+        grid=(micro, heads),
+        out_shape=(jax.ShapeDtypeStruct((micro, heads, depth, length), jnp.bfloat16),) * 3,
+        in_specs=[
+            pl.BlockSpec((1, 3, 1, depth, length), lambda m, h: (m, 0, h, 0, 0)),
+            pl.BlockSpec((1, length, 1), lambda m, h: (m, 0, 0)),
+            pl.BlockSpec((1, 1, length), lambda m, h: (m, 0, 0)),
+            head_block,
+            pl.BlockSpec((1, 1, 2, length), lambda m, h: (m, h, 0, 0)),
+            head_block,
+        ],
+        out_specs=(head_block,) * 3,
+        compiler_params=pltpu.CompilerParams(vmem_limit_bytes=VMEM_LIMIT),
+    )(qkv, seg_col, seg_row, context, stats, dcontext)
+
+
+def fast_body(
+    hidden_in,
+    segment_ids,
+    queries,
+    targets,
+    cotangent,
+    query_weight,
+    key_weight,
+    value_weight,
+    output_weight,
+    query_bias,
+    value_bias,
+    output_bias,
+    first_gain,
+    first_shift,
+    inner_weight,
+    inner_bias,
+    outer_weight,
+    outer_bias,
+    second_gain,
+    second_shift,
+):
+    dp_size, ring_size = lax.axis_size("dp"), lax.axis_size("blk")
+    dp, blk = lax.axis_index("dp"), lax.axis_index("blk")
+    micro, row_count, block_tokens, width = hidden_in.shape
+    row_queries = queries.shape[1]
+    length = block_tokens * ring_size
+    head_dim = width // HEADS
+    own_heads = HEADS // ring_size
+    score_scale = 1.0 / math.sqrt(head_dim)
+    tokens = micro * block_tokens
+    wide = jnp.float32
+    narrow = jnp.bfloat16
+
+    vectors = (
+        query_bias,
+        value_bias,
+        output_bias,
+        first_gain,
+        first_shift,
+        outer_bias,
+        second_gain,
+        second_shift,
+        inner_bias,
+    )
+    vector_size = sum(v.shape[0] for v in vectors)
+    piece = vectors[0].shape[0]
+    pack_size = -(-vector_size // 2048) * 2048
+    pack = jnp.pad(jnp.concatenate(vectors), (0, pack_size - vector_size)).reshape(-1, 128)
+    target_pack = jnp.pad(targets, ((0, 8 - micro), (0, 128 - row_queries)))
+    seg_pack = jnp.pad(segment_ids.reshape(micro, block_tokens), ((0, 8 - micro), (0, 0)))
+    shards = (
+        pack,
+        target_pack,
+        queries.reshape(micro * row_queries, width),
+        query_weight,
+        key_weight,
+        value_weight,
+        output_weight,
+        inner_weight,
+        outer_weight,
+    )
+    routes = (("x", "y"), ("y", "x"), ("x", "y")) + (("x", "y"), ("y", "x")) * 3
+    (
+        pack_all,
+        targets_all,
+        queries_all,
+        wq_full,
+        wk_full,
+        wv_full,
+        wo_full,
+        w_inner,
+        w_outer,
+        seg_all,
+    ) = gather_all(shards, routes, seg_pack, dp_size, ring_size)
+    pack_rows = pack_all.reshape(dp_size, pack_size)
+    eight = (
+        pack_rows[:, : 8 * piece].reshape(dp_size, 8, piece).transpose(1, 0, 2).reshape(8, width)
+    )
+    bq_full, bv_full, bo_full, gain_one, shift_one, b_outer, gain_two, shift_two = eight.astype(
+        wide
+    )
+    b_inner = pack_rows[:, 8 * piece : vector_size].reshape(-1).astype(wide)
+    targets_all = (
+        targets_all.reshape(dp_size, 8, 128)[:, :micro, :row_queries]
+        .transpose(1, 0, 2)
+        .reshape(micro, dp_size * row_queries)
+    )
+    queries_all = (
+        queries_all.reshape(dp_size, micro, row_queries, width)
+        .transpose(1, 0, 2, 3)
+        .reshape(micro, dp_size * row_queries, width)
+    )
+    seg_row = (
+        seg_all.reshape(ring_size, 8, block_tokens)[:, :micro]
+        .transpose(1, 0, 2)
+        .reshape(micro, 1, length)
+    )
+    seg_col = seg_row.reshape(micro, length, 1)
+
+    flat_rows = hidden_in.reshape(tokens, width)
+    rows_of = hidden_in.reshape(micro, block_tokens, width)
+
+    def projected(weight, bias=None):
+        out = jnp.einsum("mtd,de->met", rows_of, weight, preferred_element_type=wide)
+        if bias is not None:
+            out = out + bias[None, :, None]
+        return out.astype(narrow)
+
+    qkv = to_heads(
+        (projected(wq_full, bq_full), projected(wk_full), projected(wv_full, bv_full)),
+        ring_size,
+        2,
+    ).reshape(micro, 3, own_heads, head_dim, length)
+    context, context_low, stats = attend(qkv, seg_col, seg_row, score_scale)
+    (context_t,) = to_tokens(
+        (context_low.reshape(micro, own_heads * head_dim, length),), ring_size, 3
+    )
+    attended = (
+        jnp.einsum("met,ed->mtd", context_t, wo_full, preferred_element_type=wide).reshape(
+            tokens, width
+        )
+        + bo_full
+    )
+    first_out, first_normed, first_factor = layer_norm(
+        flat_rows.astype(wide) + attended, gain_one, shift_one
+    )
+    first_low = first_out.astype(narrow)
+    inner_pre = jnp.dot(first_low, w_inner, preferred_element_type=wide) + b_inner
+    active = jax.nn.gelu(inner_pre, approximate=False).astype(narrow)
+    outer_out = jnp.dot(active, w_outer, preferred_element_type=wide) + b_outer
+    output, second_normed, second_factor = layer_norm(first_out + outer_out, gain_two, shift_two)
+    output_low = output.astype(narrow)
+    output_rows = output_low.reshape(micro, block_tokens, width)
+
+    segment = segment_ids.reshape(micro, block_tokens)
+    padded = jnp.pad(seg_row.reshape(micro, length), ((0, 0), (1, 0)), constant_values=-1)
+    before = lax.dynamic_slice(padded, (0, blk * block_tokens), (micro, block_tokens))
+    numbers = jnp.arange(row_queries, dtype=jnp.int32)
+    select = (
+        (segment != before)[:, None, :] & (segment[:, None, :] == numbers[None, :, None])
+    ).astype(wide)
+    own_table = jnp.einsum(
+        "msi,mid->msd", select.astype(narrow), output_rows, preferred_element_type=wide
+    ).astype(narrow)
+    tables = gather_tables(own_table.reshape(micro * row_queries, width), ring_size, dp_size)
+    tables = tables.reshape(dp_size, micro, row_queries, width)
+    everyone = tables.transpose(1, 0, 2, 3).reshape(micro, dp_size * row_queries, width)
+    embeddings = lax.dynamic_index_in_dim(tables, dp, 0, keepdims=False)
+    query_scores = jnp.einsum("mqd,mpd->mqp", queries_all, everyone, preferred_element_type=wide)
+    score_peak = jnp.max(query_scores, axis=2, keepdims=True)
+    log_total = score_peak[..., 0] + jnp.log(jnp.sum(jnp.exp(query_scores - score_peak), axis=2))
+    target_hot = (
+        jnp.arange(query_scores.shape[2], dtype=jnp.int32)[None, None, :]
+        == targets_all[:, :, None]
+    ).astype(wide)
+    losses = log_total - jnp.sum(query_scores * target_hot, axis=2)
+    query_loss = lax.dynamic_slice(losses, (0, dp * row_queries), (micro, row_queries))
+    dscore_query = jnp.exp(query_scores - log_total[..., None]) - target_hot
+    own_dscore = lax.dynamic_slice(
+        dscore_query, (0, dp * row_queries, 0), (micro, row_queries, dp_size * row_queries)
+    )
+    query_grad = jnp.einsum("mqp,mpd->mqd", own_dscore, everyone.astype(wide), precision=PRECISE)
+    own_columns = lax.dynamic_slice(
+        dscore_query, (0, 0, dp * row_queries), (micro, dp_size * row_queries, row_queries)
+    )
+    embed_grad = jnp.einsum(
+        "mqs,mqd->msd", own_columns, queries_all.astype(wide), precision=PRECISE
+    )
+    cls_grad = jnp.einsum("msi,msd->mid", select, embed_grad, precision=PRECISE)
+    dout = cotangent.reshape(tokens, width).astype(wide) + cls_grad.reshape(tokens, width)
+    gain_two_grad = jnp.sum(dout * second_normed, axis=0)
+    shift_two_grad = jnp.sum(dout, axis=0)
+    dsecond = norm_back(dout, second_normed, second_factor, gain_two)
+    douter = dsecond.astype(narrow)
+    outer_bias_grad = jnp.sum(douter.astype(wide), axis=0)
+    outer_weight_grad = jnp.einsum(
+        "nf,nd->fd", active, douter, preferred_element_type=wide
+    ).astype(narrow)
+    dactive = jnp.einsum("nd,fd->nf", douter, w_outer, preferred_element_type=wide)
+    dinner = (dactive * gelu_slope(inner_pre)).astype(narrow)
+    inner_bias_grad = jnp.sum(dinner.astype(wide), axis=0)
+    inner_weight_grad = jnp.einsum(
+        "nd,nf->df", first_low, dinner, preferred_element_type=wide
+    ).astype(narrow)
+    dfirst = dsecond + jnp.einsum("nf,df->nd", dinner, w_inner, preferred_element_type=wide)
+    gain_one_grad = jnp.sum(dfirst * first_normed, axis=0)
+    shift_one_grad = jnp.sum(dfirst, axis=0)
+    dresidual = norm_back(dfirst, first_normed, first_factor, gain_one)
+    dattended = dresidual.astype(narrow)
+    output_bias_grad = jnp.sum(dattended.astype(wide), axis=0)
+    datt_rows = dattended.reshape(micro, block_tokens, width)
+    output_weight_grad = jnp.einsum(
+        "met,mtd->ed", context_t, datt_rows, preferred_element_type=wide
+    ).astype(narrow)
+    dcontext_t = jnp.einsum(
+        "mtd,ed->met", datt_rows, wo_full, preferred_element_type=wide
+    ).astype(narrow)
+    dcontext = to_heads((dcontext_t,), ring_size, 5).reshape(
+        micro, own_heads, head_dim, length
+    )
+    dparts = attend_back(qkv, seg_col, seg_row, context, stats, dcontext, score_scale)
+    dquery_t, dkey_t, dvalue_t = to_tokens(
+        tuple(part.reshape(micro, own_heads * head_dim, length) for part in dparts), ring_size, 6
+    )
+    dhidden = dresidual.reshape(micro, block_tokens, width)
+    for part, weight in ((dquery_t, wq_full), (dkey_t, wk_full), (dvalue_t, wv_full)):
+        dhidden = dhidden + jnp.einsum("met,de->mtd", part, weight, preferred_element_type=wide)
+    weight_grads = tuple(
+        jnp.einsum("mtd,met->de", rows_of, part, preferred_element_type=wide).astype(narrow)
+        for part in (dquery_t, dkey_t, dvalue_t)
+    )
+    query_bias_grad = jnp.sum(dquery_t.astype(wide), axis=(0, 2))
+    value_bias_grad = jnp.sum(dvalue_t.astype(wide), axis=(0, 2))
+    vector_grads = jnp.stack(
+        (
+            query_bias_grad,
+            value_bias_grad,
+            output_bias_grad,
+            gain_one_grad,
+            shift_one_grad,
+            outer_bias_grad,
+            gain_two_grad,
+            shift_two_grad,
+        )
+    )
+    grad_pack = jnp.concatenate(
+        (
+            vector_grads.reshape(8, dp_size, piece).transpose(1, 0, 2).reshape(dp_size, -1),
+            inner_bias_grad.reshape(dp_size, -1),
+            jnp.zeros((dp_size, pack_size - vector_size), wide),
+        ),
+        axis=1,
+    )
+    grad_pack = grad_pack.astype(narrow).reshape(-1, 128)
+    reduced = reduce_all(
+        (outer_weight_grad, inner_weight_grad, output_weight_grad) + weight_grads + (grad_pack,),
+        (("x", "y"), ("y", "x")) * 3 + (("x", "y"),),
+        7,
+    )
+    d_outer, d_inner, d_wo, d_wq, d_wk, d_wv, d_pack = reduced
+    d_pack = d_pack.reshape(-1)
+    small = [d_pack[i * piece : (i + 1) * piece] for i in range(8)]
+    d_bq, d_bv, d_bo, d_g1, d_s1, d_bu, d_g2, d_s2 = small
+    d_bi = d_pack[8 * piece : vector_size]
+    shape = (micro, row_count, block_tokens, width)
+    return (
+        output_low.reshape(shape),
+        embeddings,
+        query_loss,
+        query_grad,
+        dhidden.astype(narrow).reshape(shape),
+        d_wq,
+        d_wk,
+        d_wv,
+        d_wo,
+        d_bq,
+        d_bv,
+        d_bo,
+        d_g1,
+        d_s1,
+        d_inner,
+        d_bi,
+        d_outer,
+        d_bu,
+        d_g2,
+        d_s2,
+    )
+
+
 def solution(mesh):
     in_specs = (
         P(None, "dp", "blk", None),
@@ -491,4 +1335,6 @@
         P("dp"),
         P("dp"),
     )
+    fast = mesh.shape["dp"] == 8 and mesh.shape["blk"] == 4
+    body = fast_body if fast else ring_body
     return jax.shard_map(body, mesh=mesh, in_specs=in_specs, out_specs=out_specs, check_vma=False)

time: 1370 us -> 554 us (0.40)
  waiting for transfers between devices: 783 us -> 0 us
  Pallas kernels: 0 us -> 430 us
  blocking collectives: 116 us -> 0 us
  matrix products: 185 us -> 71.7 us
  local copies, waits for them, and re-layouts: 137 us -> 37.9 us
  other arithmetic: 59.6 us -> 7.79 us
  starting transfers between devices: 43.5 us -> 0 us
  between operations: 18.3 us -> 1.55 us
    pallas_call x0 -> x9, Pallas kernels: none -> 430 us  [the longest x1 154 us: reduce_all(): pl.pallas_call(functools.partial(reduce_kernel, routes), out_shape=tuple(...]
    reduce_scatter x8 -> x0, waiting for transfers between devices: 371 us -> none  [the longest x6 308 us: body(): lax.psum_scatter(as_sent(local_sum), 'dp', scatter_dimension=0, tiled=True)]
    ppermute x52 -> x0, waiting for transfers between devices: 236 us -> none  [passed_along(): return lax.ppermute(x, axis, [(i, (i + by) % size) for i in range(size)])]
    dot_general x100 -> x23, matrix products: 185 us -> 71.7 us  [the longest x1 18.2 us: fast_body(): jnp.dot(first_low, w_inner, preferred_element_type=wide) + b_inner]
    unnamed x27 -> x0, waiting for transfers between devices: 92.8 us -> none
    psum x1 -> x0, waiting for transfers between devices: 68.2 us -> none  [body(): lax.psum(as_sent(reduced), 'blk')]
    unnamed x365 -> x106, local copies, waits for them, and re-layouts: 75.2 us -> 13.2 us
    unnamed x2 -> x0, blocking collectives: 51.8 us -> none
  transfers between devices with their start and end apart: 73 -> 0, of which waited for: 47 -> 0; matrix products, arithmetic and copies ran while one was open for 20% -> 0% of each run, Pallas kernels for 0% -> 0%
where the time goes in v1:
time: 554 us; the launch traced here: 549 us
  Pallas kernels  430 us (78%)
  matrix products  71.7 us (13%)
  local copies, waits for them, and re-layouts  37.9 us (7%)
  other arithmetic  7.79 us (1%)
    pallas_call x1, Pallas kernels, reduce_all(): pl.pallas_call(functools.partial(reduce_kernel, routes), out_shape=tuple(...  154 us
    pallas_call x2, Pallas kernels, to_heads(): pl.pallas_call(functools.partial(to_heads_kernel, ring_size), out_shape=j...  74.1 us
    pallas_call x2, Pallas kernels, to_tokens(): pl.pallas_call(functools.partial(to_tokens_kernel, ring_size), out_shape=...  74 us
    pallas_call x1, Pallas kernels, gather_all(): pl.pallas_call(functools.partial(gather_kernel, routes, ring_size), out_s...  70.7 us
    pallas_call x1, Pallas kernels, attend_back(): pl.pallas_call(functools.partial(attend_back_kernel, score_scale, block),...  22.1 us
    pallas_call x1, Pallas kernels, attend(): pl.pallas_call(functools.partial(attend_kernel, score_scale, block), grid...  20.6 us
    dot_general x1, matrix products, fast_body(): jnp.dot(first_low, w_inner, preferred_element_type=wide) + b_inner  18.2 us
    pallas_call x1, Pallas kernels, gather_tables(): pl.pallas_call(functools.partial(tables_kernel, ring_size, dp_size), out_...  14.2 us

profile of v1, /device:TPU:0, one launch (start us, length us, event | category | flops | bytes accessed | tf_op | source)
XLA Modules:
  0.0 549.1 jit_solution(11414391747167403917)
XLA Ops:
  0.7 6.2 %concatenate.9 = bf16[1152]{0:T(1024)(128)(2,1)S(1)} concatenate(bf16[96]{0:T(256)(128)(2,1)} %param.29, bf16[96]{0:T(256)(128)(2,1)} %param.30, bf16[96]{0:T(256)(128)(2,1)} %param.31, bf16[96]{0:T(256)(128)(2,1)} %param.32, bf16[96]{0:T(256)(128)(2,1)} %param.33, bf16[96]{0:T(256)(128)(2,1)} %param.37, bf16[96]{0:T(256)(128)(2,1)} %param.38, bf16[96]{0:T(256)(128)(2,1)} %param.39, ...), dimensions={0} | concatenate | bytes 4608 | tf_op jit(solution)/shard_map/concatenate | solution.py:1071
  10.0 70.7 %shard_map.347 = (bf16[128,128]{1,0:T(8,128)(2,1)}, s32[64,128]{1,0:T(8,128)}, bf16[256,768]{1,0:T(8,128)(2,1)}, bf16[768,768]{1,0:T(8,128)(2,1)}, bf16[768,768]...) custom-call(bf16[16,128]{1,0:T(8,128)(2,1)} %pad_bitcast_fusion.refs, ...), custom_call_target="tpu_custom_call" | custom-call | tf_op jit(solution)/shard_map/pallas_call | solution.py:579
  81.9 3.1 fusion.23.refs_0_
  85.0 1.7 fusion.25.refs_1_
  86.8 1.7 fusion.24.refs_2_
  88.5 53.7 %shard_map.348 = bf16[2,3,192,1024]{3,2,1,0:T(8,128)(2,1)} custom-call(bf16[2,768,256]{2,1,0:T(8,128)(2,1)} %fusion.23.refs_0_, bf16[2,768,256]{2,1,0:T(8,128)(2,1)} %fusion.25.refs_1_, bf16[2,768,256]{2,1,0:T(8,128)(2,1)} %fusion.24.refs_2_), custom_call_target="tpu_custom_call" | custom-call | tf_op jit(solution)/shard_map/pallas_call | solution.py:633
  143.0 1.9 reshape_reshape.8.seg_col
  145.5 20.6 %shard_map.349 = (f32[2,3,64,1024]{3,2,1,0:T(8,128)}, bf16[2,3,64,1024]{3,2,1,0:T(8,128)(2,1)}, f32[2,3,2,1024]{3,2,1,0:T(2,128)}) custom-call(bf16[2,3,3,64,1024]{4,3,2,1,0:T(8,128)(2,1)} %bitcast.202, s32[2,1024,1]{2,1,0:T(8,128)} %reshape_reshape.8.seg_col, s32[2,1,1024]{2,1,0:T(1,128)} %reshape.306.seg_row), custom_call_target="tpu_custom_call" | custom-call | tf_op jit(solution)/shard_map/pallas_call | solution.py:954
  166.1 20.1 %shard_map.350 = bf16[2,768,256]{2,1,0:T(8,128)(2,1)} custom-call(bf16[2,192,1024]{2,1,0:T(8,128)(2,1)} %bitcast.216), custom_call_target="tpu_custom_call" | custom-call | tf_op jit(solution)/shard_map/pallas_call | solution.py:683
  186.2 2.1 fusion.46
  189.6 18.2 %fusion.2 = (bf16[512,3072]{1,0:T(8,128)(2,1)S(1)}, f32[512,3072]{1,0:T(8,128)}) fusion(f32[3072]{0:T(1024)S(1)} %reshape.329, bf16[768,3072]{1,0:T(8,128)(2,1)} %get-tuple-element.53, f32[512,768]{1,0:T(8,128)S(1)} %fusion.18, f32[768]{0:T(1024)S(1)} %add.173, f32[768]{0:T(1024)S(1)} %mul.150), kind=kOutput, calls=%fused_computation.4 | convolution fusion | flops 2520907776 | bytes 15747072 | tf_op jit(solution)/shard_map/dot_general | solution.py:1151
  207.9 6.2 %fusion.70 = (f32[512]{0:T(512)S(1)}, f32[512,768]{1,0:T(8,128)S(1)}) fusion(f32[768]{0:T(1024)S(1)} %add.178, bf16[512,3072]{1,0:T(8,128)(2,1)S(1)} %get-tuple-element.171, bf16[3072,768]{1,0:T(8,128)(2,1)} %get-tuple-element.54, f32[768]{0:T(1024)S(1)} %add.173, f32[512,768]{1,0:T(8,128)S(1)} %fusion.18, f32[768]{0:T(1024)S(1)} %mul.150), kind=kOutput, calls=%fused_computation.154 | convolution fusion | flops 2417884672 | bytes 11021312 | tf_op jit(solution)/shard_map/dot_general | solution.py:1153
  215.8 2.0 convolution_convert_fusion.4
  217.8 14.2 %shard_map.351 = bf16[8,32,768]{2,1,0:T(8,128)(2,1)} custom-call(bf16[32,768]{1,0:T(8,128)(2,1)} %bitcast.221), custom_call_target="tpu_custom_call" | custom-call | tf_op jit(solution)/shard_map/pallas_call | solution.py:727
  245.0 2.2 fusion.50
  247.5 1.9 fusion.45
  251.3 4.7 fusion.72
  256.2 3.0 multiply_reduce_fusion.1
  262.2 20.4 %shard_map.352 = bf16[2,1,192,1024]{3,2,1,0:T(8,128)(2,1)} custom-call(bf16[2,768,256]{2,1,0:T(8,128)(2,1)} %fusion.26.refs_0_), custom_call_target="tpu_custom_call" | custom-call | tf_op jit(solution)/shard_map/pallas_call | solution.py:633
  282.6 22.1 %shard_map.353 = (bf16[2,3,64,1024]{3,2,1,0:T(8,128)(2,1)}, bf16[2,3,64,1024]{3,2,1,0:T(8,128)(2,1)}, bf16[2,3,64,1024]{3,2,1,0:T(8,128)(2,1)}) custom-call(bf16[2,3,3,64,1024]{4,3,2,1,0:T(8,128)(2,1)} %bitcast.203, s32[2,1024,1]{2,1,0:T(8,128)} %reshape_reshape.8.seg_col, s32[2,1,1024]{2,1,0:T(1,128)} %reshape.306.seg_row, ...), custom_call_target="tpu_custom_call" | custom-call | tf_op jit(solution)/shard_map/pallas_call | solution.py:1006
  304.8 53.9 %shard_map.354 = (bf16[2,768,256]{2,1,0:T(8,128)(2,1)}, bf16[2,768,256]{2,1,0:T(8,128)(2,1)}, bf16[2,768,256]{2,1,0:T(8,128)(2,1)}) custom-call(bf16[2,192,1024]{2,1,0:T(8,128)(2,1)} %bitcast.217, bf16[2,192,1024]{2,1,0:T(8,128)(2,1)} %bitcast.218, bf16[2,192,1024]{2,1,0:T(8,128)(2,1)} %bitcast.219), custom_call_target="tpu_custom_call" | custom-call | tf_op jit(solution)/shard_map/pallas_call | solution.py:683
  358.7 2.5 fusion.33
  362.7 1.8 fusion.27
  365.4 4.3 convolution_convert_fusion.1.refs_0_
  369.7 4.7 convolution_convert_fusion.refs_1_
  374.5 1.8 bitcast_convert_fusion.3.refs_2_
  376.3 1.8 fusion.19.refs_3_
  378.1 1.8 fusion.20.refs_4_
  380.0 1.9 fusion.21.refs_5_
  383.8 154.3 %shard_map.355 = (f32[384,768]{1,0:T(8,128)}, f32[96,3072]{1,0:T(8,128)}, f32[96,768]{1,0:T(8,128)}, f32[96,768]{1,0:T(8,128)}, f32[96,768]{1,0:T(8,128)}, /*index=5*/f32[96,768]{1,0:T(8,128)}, f32[16,128]{1,0:T(8,128)}) custom-call(bf16[3072,768]{1,0:T(8,128)(2,1)} %convolution_convert_fusion.1.refs_0_, bf16[768,3072]{1,0:T(8,128)(2,1)} %convolution_convert_fusion.refs_1_, ...), custom_call_target="tpu_custom_call" | custom-call | tf_op jit(solution)/shard_map/pallas_call | solution.py:910
  542.7 1.7 copy.148
  544.4 1.7 copy.149
  (176 shorter events, 38.5 us)
Async XLA Ops:
  0.7 81.3 %copy-start.4 = (bf16[2,1,256,768]{3,2,1,0:T(8,128)(2,1)S(1)}, bf16[2,1,256,768]{3,2,1,0:T(8,128)(2,1)}, u32[]{:S(2)}) copy-start(bf16[2,1,256,768]{3,2,1,0:T(8,128)(2,1)} %param.20) | copy-start | bytes 2359300
  81.8 107.8 %copy-start.22 = (f32[3072]{0:T(1024)}, f32[3072]{0:T(1024)S(1)}, u32[]{:S(2)}) copy-start(f32[3072]{0:T(1024)S(1)} %reshape.329) | copy-start | bytes 36868
  81.9 3.1 copy-start.29
  166.1 20.1 %copy-start.30 = (bf16[768,768]{1,0:T(8,128)(2,1)S(1)}, bf16[768,768]{1,0:T(8,128)(2,1)}, u32[]{:S(2)}) copy-start(bf16[768,768]{1,0:T(8,128)(2,1)} %get-tuple-element.52) | copy-start | bytes 3538948
  189.5 18.3 %copy-start.26 = (f32[768]{0:T(1024)}, f32[768]{0:T(1024)S(1)}, u32[]{:S(2)}) copy-start(f32[768]{0:T(1024)S(1)} %add.173) | copy-start | bytes 9220
  189.6 18.3 %copy-start.20 = (f32[768]{0:T(1024)}, f32[768]{0:T(1024)S(1)}, u32[]{:S(2)}) copy-start(f32[768]{0:T(1024)S(1)} %mul.150) | copy-start | bytes 9220
  207.8 6.2 %copy-start.35 = (bf16[512,3072]{1,0:T(8,128)(2,1)}, bf16[512,3072]{1,0:T(8,128)(2,1)S(1)}, u32[]{:S(2)}) copy-start(bf16[512,3072]{1,0:T(8,128)(2,1)S(1)} %get-tuple-element.171) | copy-start | bytes 9437188
  215.8 17.7 %copy-start.24 = (pred[2,256]{1,0:T(4,128)(4,1)}, pred[2,256]{1,0:T(4,128)(4,1)S(1)}, u32[]{:S(2)}) copy-start(pred[2,256]{1,0:T(4,128)(4,1)S(1)} %fusion.61) | copy-start | bytes 1540
  242.7 4.8 copy-start.3
  245.0 5.8 %slice-start.4 = ((s8[6291456]{0:T(1024)(128)(4,1)}), s8[4194304]{0:T(1024)(128)(4,1)S(1)}, s32[]{:S(2)}) async-start(s8[6291456]{0:T(1024)(128)(4,1)} %bitcast.244), calls=%async_computation.4 | async-start | bytes 8388608
  247.5 3.4 slice-start.2
  249.5 1.8 slice-start.5
  250.2 5.9 %slice-start = ((s8[4718592]{0:T(1024)(128)(4,1)}), s8[4194304]{0:T(1024)(128)(4,1)S(1)}, s32[]{:S(2)}) async-start(s8[4718592]{0:T(1024)(128)(4,1)} %bitcast.240), calls=%async_computation | async-start | bytes 8388608
  250.8 5.3 copy-start.6
  251.3 4.8 copy-start.21
  251.3 4.8 slice-start.1
  256.1 3.1 copy-start.33
  256.1 3.1 copy-start.19
  358.7 2.5 copy-start.15
  358.7 2.5 copy-start.28
  362.7 1.8 copy-start.7
  362.7 2.6 copy-start.36
  365.4 4.3 copy-start.27
  365.4 4.3 copy-start.34
  369.7 4.7 copy-start.13
  369.7 4.7 copy-start.14
  374.5 1.8 copy-start.5
  376.3 1.9 copy-start.32
  380.0 1.9 copy-start.16
  380.0 2.2 copy-start.2
  538.1 8.0 %copy-start.17 = (f32[96,768]{1,0:T(8,128)S(1)}, f32[96,768]{1,0:T(8,128)}, u32[]{:S(2)}) copy-start(f32[96,768]{1,0:T(8,128)} %get-tuple-element.211) | copy-start | bytes 884740
  538.1 8.7 %copy-start.11 = (f32[96,3072]{1,0:T(8,128)S(1)}, f32[96,3072]{1,0:T(8,128)}, u32[]{:S(2)}) copy-start(f32[96,3072]{1,0:T(8,128)} %get-tuple-element.217) | copy-start | bytes 3538948
  (11 other events, 13.4 us)

commit v2 on v1

--- a/solution.py
+++ b/solution.py
@@ -495,18 +495,72 @@
 IN_VMEM = pl.BlockSpec(memory_space=pltpu.VMEM)
 
 
-def gather_kernel(routes, ring_size, *refs):
-    count = len(routes)
-    shards, seg_shard = refs[:count], refs[count]
-    fulls, seg_full = refs[count + 1 : 2 * count + 1], refs[2 * count + 1]
-    send_sem, recv_sem, seg_send, seg_recv, local_sem = refs[2 * count + 2 :]
+def window_start(blk, group, window):
+    return pl.multiple_of((blk * group) // 128 * 128, 128)
+
+
+def gather_kernel(items, ring_size, *refs):
+    count = 1 + max(item["source"] for item in items)
+    places = 1 + max(item["target"] for item in items)
+    shards, seg_shard, hidden = refs[:count], refs[count], refs[count + 1]
+    fulls = refs[count + 2 : count + 2 + places]
+    seg_full, hidden_full = refs[count + 2 + places : count + 4 + places]
+    (
+        send_sem,
+        recv_sem,
+        seg_send,
+        seg_recv,
+        line_send,
+        line_recv,
+        local_sem,
+        line_local,
+    ) = refs[count + 4 + places :]
     dp, blk, bits = place()
     sibling = across(dp, blk, bits, "c")
     ring = [(dp, lax.rem(blk + step, ring_size)) for step in range(1, ring_size)]
     greet([sibling, across(dp, blk, bits, "x"), across(dp, blk, bits, "y")] + ring)
     seg_rows = seg_shard.shape[0]
-    started = []
-    locals_started = []
+    micro, tokens, _ = hidden.shape
+    waiting = []
+    sending = []
+
+    def line_copy(m, side, distance):
+        away = 1 - 2 * side
+        owner = blk + away * distance
+        view = hidden_full.at[m, pl.ds(pl.multiple_of(owner * tokens, tokens), tokens)]
+        return remote(
+            hidden.at[m] if distance == 0 else view,
+            view,
+            line_send.at[m, side, distance],
+            line_recv.at[m, side, distance + 1],
+            (dp, blk - away),
+        )
+
+    def arrival(m, side, distance):
+        away = 1 - 2 * side
+        owner = blk + away * distance
+        view = hidden_full.at[m, pl.ds(pl.multiple_of(owner * tokens, tokens), tokens)]
+        return remote(
+            view,
+            view,
+            line_send.at[m, side, distance],
+            line_recv.at[m, side, distance],
+            (dp, blk - away),
+        )
+
+    def can_send(side):
+        return blk > 0 if side == 0 else blk < ring_size - 1
+
+    def exists(side, distance):
+        return blk + distance < ring_size if side == 0 else blk >= distance
+
+    for m in range(micro):
+        for side in range(2):
+
+            @pl.when(can_send(side))
+            def _():
+                line_copy(m, side, 0).start()
+
     for step, peer in enumerate(ring):
         copy = remote(
             seg_shard,
@@ -516,24 +570,45 @@
             peer,
         )
         copy.start()
-        started.append(copy)
+        waiting.append(copy)
     copy = pltpu.make_async_copy(
-        seg_shard, seg_full.at[pl.ds(blk * seg_rows, seg_rows)], local_sem.at[count]
+        seg_shard, seg_full.at[pl.ds(blk * seg_rows, seg_rows)], local_sem.at[len(items)]
     )
     copy.start()
-    locals_started.append(copy)
+    waiting.append(copy)
+    for m in range(micro):
+        copy = pltpu.make_async_copy(
+            hidden.at[m],
+            hidden_full.at[m, pl.ds(pl.multiple_of(blk * tokens, tokens), tokens)],
+            line_local.at[m],
+        )
+        copy.start()
+        waiting.append(copy)
+
+    def own_part(item):
+        spec = items[item]
+        column = spec["from_column"]
+        if column is None:
+            column = window_start(blk, spec["group"], spec["columns"])
+        return shards[spec["source"]].at[
+            pl.ds(spec["row"], spec["rows"]), pl.ds(column, spec["columns"])
+        ]
 
     def block(item, owner):
-        rows = shards[item].shape[0]
-        return fulls[item].at[pl.ds(owner * rows, rows)]
+        spec = items[item]
+        first = owner * spec["stride"] + spec["row"]
+        return fulls[spec["target"]].at[
+            pl.ds(first, spec["rows"]), pl.ds(spec["to_column"], spec["columns"])
+        ]
 
     inbound = {}
-    for item, (first, second) in enumerate(routes):
+    for item, spec in enumerate(items):
+        first, second = spec["route"]
         for slot, peer in enumerate(
             (across(dp, blk, bits, first), across(dp, blk, bits, second), sibling)
         ):
             copy = remote(
-                shards[item],
+                own_part(item),
                 block(item, dp),
                 send_sem.at[item, slot],
                 recv_sem.at[item, slot],
@@ -541,60 +616,101 @@
             )
             copy.start()
             inbound[item, slot] = copy
-        copy = pltpu.make_async_copy(shards[item], block(item, dp), local_sem.at[item])
+        copy = pltpu.make_async_copy(own_part(item), block(item, dp), local_sem.at[item])
         copy.start()
-        locals_started.append(copy)
-    for item, (first, second) in enumerate(routes):
+        waiting.append(copy)
+
+    def line_step(m, distance):
+        for side in range(2):
+
+            @pl.when(exists(side, distance))
+            def _():
+                arrival(m, side, distance).wait_recv()
+
+            if distance < ring_size - 1:
+
+                @pl.when(exists(side, distance) & can_send(side))
+                def _():
+                    line_copy(m, side, distance).start()
+
+    def relay_first(item):
+        first, second = items[item]["route"]
         inbound[item, 0].wait_recv()
         held = block(item, across(dp, blk, bits, first)[0])
         for slot, peer in ((3, across(dp, blk, bits, second)), (4, sibling)):
             copy = remote(held, held, send_sem.at[item, slot], recv_sem.at[item, slot], peer)
             copy.start()
             inbound[item, slot] = copy
-    for item, (first, second) in enumerate(routes):
+
+    def relay_second(item):
+        first, second = items[item]["route"]
         inbound[item, 1].wait_recv()
         held = block(item, across(dp, blk, bits, second)[0])
         copy = remote(held, held, send_sem.at[item, 5], recv_sem.at[item, 5], sibling)
         copy.start()
         inbound[item, 5] = copy
-    for item, (first, second) in enumerate(routes):
+
+    def relay_third(item):
+        first, second = items[item]["route"]
         inbound[item, 3].wait_recv()
         held = block(item, across(dp, blk, bits, first, second)[0])
         copy = remote(held, held, send_sem.at[item, 6], recv_sem.at[item, 6], sibling)
         copy.start()
         inbound[item, 6] = copy
-    for item in range(count):
+
+    steps = [(m, distance) for m in range(micro) for distance in range(1, ring_size)]
+    total = len(items) + 3
+    done = 0
+    for tick in range(total):
+        if tick < len(items):
+            relay_first(tick)
+            relay_second(tick)
+        if 0 <= tick - 3 < len(items):
+            relay_third(tick - 3)
+        while done < len(steps) and done * total < len(steps) * (tick + 1):
+            line_step(*steps[done])
+            done += 1
+    for item in range(len(items)):
         for slot in (2, 4, 5, 6):
             inbound[item, slot].wait_recv()
         for slot in range(7):
             inbound[item, slot].wait_send()
-    for copy in started:
+    for m in range(micro):
+        for side in range(2):
+            for distance in range(ring_size - 1):
+
+                @pl.when(exists(side, distance) & can_send(side))
+                def _():
+                    line_copy(m, side, distance).wait_send()
+
+    for copy in waiting:
         copy.wait()
-    for copy in locals_started:
-        copy.wait()
-
-
-def gather_all(shards, routes, segments, dp_size, ring_size):
+
+
+def gather_all(shards, items, targets, segments, hidden, ring_size):
+    micro, tokens, width = hidden.shape
     count = len(shards)
     return pl.pallas_call(
-        functools.partial(gather_kernel, routes, ring_size),
-        out_shape=tuple(
-            jax.ShapeDtypeStruct((dp_size * s.shape[0], s.shape[1]), s.dtype) for s in shards
-        )
+        functools.partial(gather_kernel, items, ring_size),
+        out_shape=tuple(targets)
         + (
             jax.ShapeDtypeStruct((ring_size * segments.shape[0], segments.shape[1]), jnp.int32),
+            jax.ShapeDtypeStruct((micro, ring_size * tokens, width), hidden.dtype),
         ),
-        in_specs=[ANY] * (count + 1),
-        out_specs=(ANY,) * (count + 1),
+        in_specs=[ANY] * (count + 2),
+        out_specs=(ANY,) * (len(targets) + 2),
         scratch_shapes=[
-            pltpu.SemaphoreType.DMA((count, 7)),
-            pltpu.SemaphoreType.DMA((count, 7)),
+            pltpu.SemaphoreType.DMA((len(items), 7)),
+            pltpu.SemaphoreType.DMA((len(items), 7)),
             pltpu.SemaphoreType.DMA((ring_size,)),
             pltpu.SemaphoreType.DMA((ring_size,)),
-            pltpu.SemaphoreType.DMA((count + 1,)),
+            pltpu.SemaphoreType.DMA((micro, 2, ring_size)),
+            pltpu.SemaphoreType.DMA((micro, 2, ring_size)),
+            pltpu.SemaphoreType.DMA((len(items) + 1,)),
+            pltpu.SemaphoreType.DMA((micro,)),
         ],
         compiler_params=comm_params(1),
-    )(*shards, segments)
+    )(*shards, segments, hidden)
 
 
 def to_heads_kernel(ring_size, *refs):
@@ -740,142 +856,161 @@
     )(own)
 
 
-def reduce_kernel(routes, *refs):
-    count = len(routes)
-    grads, outs = refs[:count], refs[count : 2 * count]
-    buffers = refs[2 * count : 2 * count + 7 * count]
-    own = buffers[:count]
-    from_core = buffers[count : 2 * count]
-    from_first = buffers[2 * count : 3 * count]
-    from_second = buffers[3 * count : 4 * count]
-    ring_one = buffers[4 * count : 5 * count]
-    ring_two = buffers[5 * count : 6 * count]
-    ring_three = buffers[6 * count : 7 * count]
-    send_sem, recv_sem, local_sem = refs[9 * count :]
+def added(left, right):
+    return (left.astype(jnp.float32) + right.astype(jnp.float32)).astype(jnp.bfloat16)
+
+
+def reduce_kernel(items, ring_size, *refs):
+    count = len(items)
+    inputs = 1 + max(item["source"] for item in items)
+    grads, outs = refs[:inputs], refs[inputs : 2 * inputs]
+    own, from_core, from_first, from_second, ring_one, ring_two, ring_three = refs[
+        2 * inputs : 2 * inputs + 7
+    ]
+    send_sem, recv_sem, local_sem = refs[2 * inputs + 7 :]
     dp, blk, bits = place()
     sibling = across(dp, blk, bits, "c")
     is_end = (blk == 0) | (blk == 3)
     is_middle = (blk == 1) | (blk == 2)
     partner = (dp, blk + 1 - 2 * lax.rem(blk, 2))
     facing = (dp, 3 - blk)
-    greet(
-        [
-            sibling,
-            across(dp, blk, bits, "x"),
-            across(dp, blk, bits, "y"),
-            partner,
-            facing,
-        ]
-    )
-    sent = []
+    ring = [(dp, lax.rem(blk + step, ring_size)) for step in range(1, ring_size)]
+    greet([sibling, across(dp, blk, bits, "x"), across(dp, blk, bits, "y")] + ring)
 
     def owner(core, axes, first_bit, second_bit):
         return core + SIDE[axes[0]] * first_bit + SIDE[axes[1]] * second_bit
 
     def block(item, which):
-        rows = grads[item].shape[0] // 8
-        return grads[item].at[pl.ds(which * rows, rows)]
+        spec = items[item]
+        return grads[spec["source"]].at[
+            pl.ds(which * spec["stride"] + spec["row"], spec["rows"]),
+            pl.ds(spec["column"], spec["columns"]),
+        ]
+
+    def cut(buffer, item, *index):
+        spec = items[item]
+        return buffer.at[(item,) + index + (pl.ds(0, spec["rows"]), pl.ds(0, spec["columns"]))]
+
+    def result(item):
+        spec = items[item]
+        return outs[spec["source"]].at[
+            pl.ds(spec["row"], spec["rows"]), pl.ds(spec["column"], spec["columns"])
+        ]
+
+    def copier(source, target, item, slot, peer):
+        return remote(source, target, send_sem.at[item, slot], recv_sem.at[item, slot], peer)
 
     def go(source, target, item, slot, peer):
-        copy = remote(source, target, send_sem.at[item, slot], recv_sem.at[item, slot], peer)
+        copy = copier(source, target, item, slot, peer)
         copy.start()
         return copy
 
     flying = {}
 
     def start_core(item):
-        axes = routes[item]
+        axes = items[item]["route"]
         for f in range(2):
             for s in range(2):
-                copy = go(
+                slot = 2 * f + s
+                flying[item, slot] = go(
                     block(item, owner(1 - bits["c"], axes, f, s)),
-                    from_core[item].at[f, s],
+                    cut(from_core, item, f, s),
                     item,
-                    2 * f + s,
+                    slot,
                     sibling,
                 )
-                flying[item, 2 * f + s] = copy
                 mine = pltpu.make_async_copy(
                     block(item, owner(bits["c"], axes, f, s)),
-                    own[item].at[f, s],
-                    local_sem.at[item, 2 * f + s],
+                    cut(own, item, f, s),
+                    local_sem.at[item, slot],
                 )
                 mine.start()
-                flying[item, "own", 2 * f + s] = mine
-
-    def added(left, right):
-        return (left.astype(jnp.float32) + right.astype(jnp.float32)).astype(jnp.bfloat16)
+                flying[item, "own", slot] = mine
 
     def after_core(item):
-        axes = routes[item]
+        axes = items[item]["route"]
         mine = bits[axes[0]]
         for slot in range(4):
             flying[item, slot].wait_recv()
             flying[item, "own", slot].wait()
         for f in (1 - mine, mine):
             for s in range(2):
-                own[item][f, s] = added(own[item][f, s], from_core[item][f, s])
+                part = cut(own, item, f, s)
+                part[...] = added(part[...], cut(from_core, item, f, s)[...])
                 if f is not mine:
                     flying[item, 4 + s] = go(
-                        own[item].at[f, s],
-                        from_first[item].at[s],
+                        part,
+                        cut(from_first, item, s),
                         item,
                         4 + s,
                         across(dp, blk, bits, axes[0]),
                     )
 
     def after_first(item):
-        axes = routes[item]
+        axes = items[item]["route"]
         f, mine = bits[axes[0]], bits[axes[1]]
         for s in range(2):
             flying[item, 4 + s].wait_recv()
-        own[item][f, 1 - mine] = added(own[item][f, 1 - mine], from_first[item][1 - mine])
+        part = cut(own, item, f, 1 - mine)
+        part[...] = added(part[...], cut(from_first, item, 1 - mine)[...])
         flying[item, 6] = go(
-            own[item].at[f, 1 - mine],
-            from_second[item],
-            item,
-            6,
-            across(dp, blk, bits, axes[1]),
-        )
-        own[item][f, mine] = added(own[item][f, mine], from_first[item][mine])
+            part, cut(from_second, item), item, 6, across(dp, blk, bits, axes[1])
+        )
+        part = cut(own, item, f, mine)
+        part[...] = added(part[...], cut(from_first, item, mine)[...])
 
     def after_second(item):
-        axes = routes[item]
+        axes = items[item]["route"]
         f, s = bits[axes[0]], bits[axes[1]]
         flying[item, 6].wait_recv()
-        ring_one[item][0] = added(own[item][f, s], from_second[item][...])
-
-        def ring_copy(source, target, slot, peer):
-            return remote(source, target, send_sem.at[item, slot], recv_sem.at[item, slot], peer)
-
-        flying[item, 7] = ring_copy(ring_one[item].at[0], ring_one[item].at[1], 7, partner)
-        flying[item, 8] = ring_copy(ring_two[item].at[0], ring_two[item].at[1], 8, facing)
-        flying[item, 9] = ring_copy(ring_three[item].at[0], ring_three[item].at[1], 9, partner)
+        total = added(cut(own, item, f, s)[...], cut(from_second, item)[...])
+        if items[item]["gathered"]:
+            out = outs[items[item]["source"]]
+            out[blk] = total
+            for step, peer in enumerate(ring):
+                flying[item, 7 + step] = go(out.at[blk], out.at[blk], item, 7 + step, peer)
+            return
+        cut(ring_one, item, 0)[...] = total
+        flying[item, 7] = copier(
+            cut(ring_one, item, 0), cut(ring_one, item, 1), item, 7, partner
+        )
+        flying[item, 8] = copier(cut(ring_two, item, 0), cut(ring_two, item, 1), item, 8, facing)
+        flying[item, 9] = copier(result(item), result(item), item, 9, partner)
 
         @pl.when(is_end)
         def _():
             flying[item, 7].start()
 
     def at_middle(item):
+        if items[item]["gathered"]:
+            return
+
         @pl.when(is_middle)
         def _():
             flying[item, 7].wait_recv()
-            ring_two[item][0] = added(ring_one[item][0], ring_one[item][1])
+            part = cut(ring_two, item, 0)
+            part[...] = added(cut(ring_one, item, 0)[...], cut(ring_one, item, 1)[...])
             flying[item, 8].start()
 
     def across_middle(item):
+        if items[item]["gathered"]:
+            return
+
         @pl.when(is_middle)
         def _():
             flying[item, 8].wait_recv()
-            ring_three[item][0] = added(ring_two[item][0], ring_two[item][1])
+            result(item)[...] = added(cut(ring_two, item, 0)[...], cut(ring_two, item, 1)[...])
             flying[item, 9].start()
-            outs[item][...] = ring_three[item][0].astype(jnp.float32)
 
     def at_end(item):
+        if items[item]["gathered"]:
+            for step in range(ring_size - 1):
+                flying[item, 7 + step].wait_recv()
+            return
+
         @pl.when(is_end)
         def _():
             flying[item, 9].wait_recv()
-            outs[item][...] = ring_three[item][1].astype(jnp.float32)
 
     stages = (after_core, after_first, after_second, at_middle, across_middle, at_end)
     for item in range(count):
@@ -888,30 +1023,45 @@
     for item in range(count):
         for slot in range(7):
             flying[item, slot].wait_send()
+        if items[item]["gathered"]:
+            for step in range(ring_size - 1):
+                flying[item, 7 + step].wait_send()
 
     @pl.when(is_end)
     def _():
         for item in range(count):
-            flying[item, 7].wait_send()
+            if not items[item]["gathered"]:
+                flying[item, 7].wait_send()
 
     @pl.when(is_middle)
     def _():
         for item in range(count):
-            flying[item, 8].wait_send()
-            flying[item, 9].wait_send()
-
-
-def reduce_all(grads, routes, collective):
-    count = len(grads)
-    shards = [(g.shape[0] // 8, g.shape[1]) for g in grads]
-    scratch = []
-    for lead in ((2, 2), (2, 2), (2,), (), (2,), (2,), (2,)):
-        scratch += [pltpu.VMEM(lead + shard, jnp.bfloat16) for shard in shards]
+            if not items[item]["gathered"]:
+                flying[item, 8].wait_send()
+                flying[item, 9].wait_send()
+
+
+def reduce_all(grads, items, dp_size, ring_size, collective):
+    count = len(items)
+    inputs = len(grads)
+    rows = max(item["rows"] for item in items)
+    columns = max(item["columns"] for item in items)
+    piece = (rows, columns)
+    outs = []
+    for index, grad in enumerate(grads):
+        shard = (grad.shape[0] // dp_size, grad.shape[1])
+        if any(item["gathered"] for item in items if item["source"] == index):
+            shard = (ring_size,) + shard
+        outs.append(jax.ShapeDtypeStruct(shard, jnp.bfloat16))
+    scratch = [
+        pltpu.VMEM((count,) + lead + piece, jnp.bfloat16)
+        for lead in ((2, 2), (2, 2), (2,), (), (2,), (2,), (2,))
+    ]
     return pl.pallas_call(
-        functools.partial(reduce_kernel, routes),
-        out_shape=tuple(jax.ShapeDtypeStruct(shard, jnp.float32) for shard in shards),
-        in_specs=[ANY] * count,
-        out_specs=(IN_VMEM,) * count,
+        functools.partial(reduce_kernel, items, ring_size),
+        out_shape=tuple(outs),
+        in_specs=[ANY] * inputs,
+        out_specs=(IN_VMEM,) * inputs,
         scratch_shapes=scratch
         + [
             pltpu.SemaphoreType.DMA((count, 10)),
@@ -920,6 +1070,109 @@
         ],
         compiler_params=comm_params(collective),
     )(*grads)
+
+
+def scatter_line_kernel(ring_size, parts, out, passed, arrived, send_sem, recv_sem):
+    dp, blk, _ = place()
+    greet_line(dp, blk, ring_size)
+    micro, _, tokens, _ = parts.shape
+
+    def can_receive(side):
+        return blk < ring_size - 1 if side == 0 else blk > 0
+
+    def has_target(side, distance):
+        return blk >= distance if side == 0 else blk + distance < ring_size
+
+    def hop(source, m, side, distance):
+        return remote(
+            source,
+            arrived.at[m, side, distance - 1],
+            send_sem.at[m, side, distance],
+            recv_sem.at[m, side, distance - 1],
+            (dp, blk - 1 + 2 * side),
+        )
+
+    def arrival(m, side, distance):
+        view = arrived.at[m, side, distance]
+        return remote(
+            view,
+            view,
+            send_sem.at[m, side, distance],
+            recv_sem.at[m, side, distance],
+            (dp, blk - 1 + 2 * side),
+        )
+
+    for distance in reversed(range(1, ring_size)):
+        for m in range(micro):
+            for side in range(2):
+                target = blk - distance * (1 - 2 * side)
+                if distance < ring_size - 1:
+
+                    @pl.when(has_target(side, distance) & can_receive(side))
+                    def _():
+                        arrival(m, side, distance).wait_recv()
+                        passed[m, side, distance] = added(
+                            parts[m, target], arrived[m, side, distance]
+                        )
+                        hop(passed.at[m, side, distance], m, side, distance).start()
+
+                @pl.when(has_target(side, distance) & jnp.logical_not(can_receive(side)))
+                def _():
+                    hop(parts.at[m, target], m, side, distance).start()
+
+    for m in range(micro):
+        out[m] = parts[m, blk].astype(jnp.float32)
+        for side in range(2):
+
+            @pl.when(can_receive(side))
+            def _():
+                arrival(m, side, 0).wait_recv()
+                out[m] += arrived[m, side, 0].astype(jnp.float32)
+
+    for distance in range(1, ring_size):
+        for m in range(micro):
+            for side in range(2):
+
+                @pl.when(has_target(side, distance))
+                def _():
+                    hop(passed.at[m, side, distance], m, side, distance).wait_send()
+
+
+def greet_line(dp, blk, ring_size):
+    barrier = pltpu.get_barrier_semaphore()
+
+    @pl.when(blk > 0)
+    def _():
+        pl.semaphore_signal(barrier, inc=1, device_id=(dp, blk - 1), device_id_type=MESH)
+
+    @pl.when(blk < ring_size - 1)
+    def _():
+        pl.semaphore_signal(barrier, inc=1, device_id=(dp, blk + 1), device_id_type=MESH)
+
+    @pl.when((blk > 0) & (blk < ring_size - 1))
+    def _():
+        pl.semaphore_wait(barrier, 2)
+
+    @pl.when((blk == 0) | (blk == ring_size - 1))
+    def _():
+        pl.semaphore_wait(barrier, 1)
+
+
+def scatter_line(parts, ring_size, collective):
+    micro, _, tokens, width = parts.shape
+    return pl.pallas_call(
+        functools.partial(scatter_line_kernel, ring_size),
+        out_shape=jax.ShapeDtypeStruct((micro, tokens, width), jnp.float32),
+        in_specs=[IN_VMEM],
+        out_specs=IN_VMEM,
+        scratch_shapes=[
+            pltpu.VMEM((micro, 2, ring_size, tokens, width), jnp.bfloat16),
+            pltpu.VMEM((micro, 2, ring_size, tokens, width), jnp.bfloat16),
+            pltpu.SemaphoreType.DMA((micro, 2, ring_size)),
+            pltpu.SemaphoreType.DMA((micro, 2, ring_size)),
+        ],
+        compiler_params=comm_params(collective),
+    )(parts)
 
 
 def contract(left, right, left_dim, right_dim):
@@ -1065,44 +1318,78 @@
         second_shift,
         inner_bias,
     )
-    vector_size = sum(v.shape[0] for v in vectors)
     piece = vectors[0].shape[0]
-    pack_size = -(-vector_size // 2048) * 2048
-    pack = jnp.pad(jnp.concatenate(vectors), (0, pack_size - vector_size)).reshape(-1, 128)
+    inner_piece = inner_bias.shape[0]
+    group = own_heads * head_dim
+    window = -(-group // 128) * 128
+    window_heads = window // head_dim
+    hidden_rows = hidden_in.reshape(micro, block_tokens, width)
+    pack = jnp.concatenate(
+        (
+            jnp.pad(jnp.stack(vectors[:8]), ((0, 0), (0, inner_piece - piece))),
+            jnp.pad(inner_bias[None], ((0, 7), (0, 0))),
+        )
+    )
     target_pack = jnp.pad(targets, ((0, 8 - micro), (0, 128 - row_queries)))
     seg_pack = jnp.pad(segment_ids.reshape(micro, block_tokens), ((0, 8 - micro), (0, 0)))
     shards = (
+        query_weight,
+        key_weight,
+        value_weight,
         pack,
         target_pack,
         queries.reshape(micro * row_queries, width),
-        query_weight,
-        key_weight,
-        value_weight,
         output_weight,
         inner_weight,
         outer_weight,
     )
-    routes = (("x", "y"), ("y", "x"), ("x", "y")) + (("x", "y"), ("y", "x")) * 3
+    ways = (("x", "y"), ("y", "x"))
+    items = []
+
+    def add_item(source, target, row=0, rows=None, from_column=0, columns=None, to_column=0):
+        shape = shards[source].shape
+        items.append(
+            {
+                "source": source,
+                "target": target,
+                "row": row,
+                "rows": rows or shape[0],
+                "stride": shape[0],
+                "from_column": from_column,
+                "columns": columns or shape[1],
+                "to_column": to_column,
+                "group": group,
+                "route": ways[len(items) % 2],
+            }
+        )
+
+    for index in range(3):
+        add_item(index, 0, from_column=None, columns=window, to_column=index * window)
+    for index in range(3, 7):
+        add_item(index, index - 2)
+    for part in range(4):
+        add_item(
+            7, 5, from_column=part * width, columns=width, to_column=part * width
+        )
+        add_item(8, 6, row=part * piece, rows=piece)
+    targets_out = [jax.ShapeDtypeStruct((width, 3 * window), narrow)] + [
+        jax.ShapeDtypeStruct((dp_size * s.shape[0], s.shape[1]), s.dtype) for s in shards[3:]
+    ]
     (
+        w_window,
         pack_all,
         targets_all,
         queries_all,
-        wq_full,
-        wk_full,
-        wv_full,
         wo_full,
         w_inner,
         w_outer,
         seg_all,
-    ) = gather_all(shards, routes, seg_pack, dp_size, ring_size)
-    pack_rows = pack_all.reshape(dp_size, pack_size)
-    eight = (
-        pack_rows[:, : 8 * piece].reshape(dp_size, 8, piece).transpose(1, 0, 2).reshape(8, width)
-    )
-    bq_full, bv_full, bo_full, gain_one, shift_one, b_outer, gain_two, shift_two = eight.astype(
-        wide
-    )
-    b_inner = pack_rows[:, 8 * piece : vector_size].reshape(-1).astype(wide)
+        hidden_all,
+    ) = gather_all(shards, items, targets_out, seg_pack, hidden_rows, ring_size)
+    pack_rows = pack_all.reshape(dp_size, 16, inner_piece)
+    eight = pack_rows[:, :8, :piece].transpose(1, 0, 2).reshape(8, width).astype(wide)
+    bq_full, bv_full, bo_full, gain_one, shift_one, b_outer, gain_two, shift_two = eight
+    b_inner = pack_rows[:, 8].reshape(-1).astype(wide)
     targets_all = (
         targets_all.reshape(dp_size, 8, 128)[:, :micro, :row_queries]
         .transpose(1, 0, 2)
@@ -1121,19 +1408,24 @@
     seg_col = seg_row.reshape(micro, length, 1)
 
     flat_rows = hidden_in.reshape(tokens, width)
-    rows_of = hidden_in.reshape(micro, block_tokens, width)
-
-    def projected(weight, bias=None):
-        out = jnp.einsum("mtd,de->met", rows_of, weight, preferred_element_type=wide)
-        if bias is not None:
-            out = out + bias[None, :, None]
-        return out.astype(narrow)
-
-    qkv = to_heads(
-        (projected(wq_full, bq_full), projected(wk_full), projected(wv_full, bv_full)),
-        ring_size,
-        2,
-    ).reshape(micro, 3, own_heads, head_dim, length)
+    window_at = (blk * group) // 128 * 128
+    head_at = (blk * group - window_at) // head_dim
+    bias_window = jnp.concatenate(
+        (
+            lax.dynamic_slice(bq_full, (window_at,), (window,)),
+            jnp.zeros((window,), wide),
+            lax.dynamic_slice(bv_full, (window_at,), (window,)),
+        )
+    )
+    qkv_window = (
+        jnp.einsum("mtd,de->met", hidden_all, w_window, preferred_element_type=wide)
+        + bias_window[None, :, None]
+    ).astype(narrow)
+    qkv = lax.dynamic_slice(
+        qkv_window.reshape(micro, 3, window_heads, head_dim, length),
+        (0, 0, head_at, 0, 0),
+        (micro, 3, own_heads, head_dim, length),
+    )
     context, context_low, stats = attend(qkv, seg_col, seg_row, score_scale)
     (context_t,) = to_tokens(
         (context_low.reshape(micro, own_heads * head_dim, length),), ring_size, 3
@@ -1222,18 +1514,26 @@
         micro, own_heads, head_dim, length
     )
     dparts = attend_back(qkv, seg_col, seg_row, context, stats, dcontext, score_scale)
-    dquery_t, dkey_t, dvalue_t = to_tokens(
-        tuple(part.reshape(micro, own_heads * head_dim, length) for part in dparts), ring_size, 6
-    )
-    dhidden = dresidual.reshape(micro, block_tokens, width)
-    for part, weight in ((dquery_t, wq_full), (dkey_t, wk_full), (dvalue_t, wv_full)):
-        dhidden = dhidden + jnp.einsum("met,de->mtd", part, weight, preferred_element_type=wide)
-    weight_grads = tuple(
-        jnp.einsum("mtd,met->de", rows_of, part, preferred_element_type=wide).astype(narrow)
-        for part in (dquery_t, dkey_t, dvalue_t)
-    )
-    query_bias_grad = jnp.sum(dquery_t.astype(wide), axis=(0, 2))
-    value_bias_grad = jnp.sum(dvalue_t.astype(wide), axis=(0, 2))
+    dwindow = jnp.stack(dparts, axis=1)
+    dwindow = lax.dynamic_update_slice(
+        jnp.zeros((micro, 3, window_heads, head_dim, length), narrow), dwindow, (0, 0, head_at, 0, 0)
+    ).reshape(micro, 3 * window, length)
+    dhidden_parts = jnp.einsum(
+        "met,de->mtd", dwindow, w_window, preferred_element_type=wide
+    ).astype(narrow)
+    dhidden = dresidual.reshape(micro, block_tokens, width) + scatter_line(
+        dhidden_parts.reshape(micro, ring_size, block_tokens, width), ring_size, 6
+    )
+    window_grad = jnp.einsum(
+        "mtd,met->de", hidden_all, dwindow, preferred_element_type=wide
+    ).astype(narrow)
+    bias_grads = jnp.sum(dwindow.astype(wide), axis=(0, 2))
+    query_bias_grad, value_bias_grad = (
+        lax.dynamic_update_slice(
+            jnp.zeros((width,), wide), bias_grads[at : at + window], (window_at,)
+        )
+        for at in (0, 2 * window)
+    )
     vector_grads = jnp.stack(
         (
             query_bias_grad,
@@ -1245,26 +1545,58 @@
             gain_two_grad,
             shift_two_grad,
         )
-    )
-    grad_pack = jnp.concatenate(
-        (
-            vector_grads.reshape(8, dp_size, piece).transpose(1, 0, 2).reshape(dp_size, -1),
-            inner_bias_grad.reshape(dp_size, -1),
-            jnp.zeros((dp_size, pack_size - vector_size), wide),
+    ).astype(narrow)
+    grad_pack = jnp.pad(
+        jnp.concatenate(
+            (
+                jnp.pad(
+                    vector_grads.reshape(8, dp_size, piece).transpose(1, 0, 2),
+                    ((0, 0), (0, 0), (0, inner_piece - piece)),
+                ),
+                inner_bias_grad.astype(narrow).reshape(dp_size, 1, inner_piece),
+            ),
+            axis=1,
         ),
-        axis=1,
-    )
-    grad_pack = grad_pack.astype(narrow).reshape(-1, 128)
-    reduced = reduce_all(
-        (outer_weight_grad, inner_weight_grad, output_weight_grad) + weight_grads + (grad_pack,),
-        (("x", "y"), ("y", "x")) * 3 + (("x", "y"),),
-        7,
-    )
-    d_outer, d_inner, d_wo, d_wq, d_wk, d_wv, d_pack = reduced
-    d_pack = d_pack.reshape(-1)
-    small = [d_pack[i * piece : (i + 1) * piece] for i in range(8)]
-    d_bq, d_bv, d_bo, d_g1, d_s1, d_bu, d_g2, d_s2 = small
-    d_bi = d_pack[8 * piece : vector_size]
+        ((0, 0), (0, 7), (0, 0)),
+    ).reshape(dp_size * 16, inner_piece)
+    grads = (outer_weight_grad, inner_weight_grad, output_weight_grad, window_grad, grad_pack)
+    sums = []
+
+    def add_sum(source, row=0, rows=None, column=0, columns=None, gathered=False):
+        shape = grads[source].shape
+        sums.append(
+            {
+                "source": source,
+                "row": row,
+                "rows": rows or shape[0] // dp_size,
+                "stride": shape[0] // dp_size,
+                "column": column,
+                "columns": columns or shape[1],
+                "gathered": gathered,
+                "route": ways[len(sums) % 2],
+            }
+        )
+
+    for part in range(4):
+        add_sum(0, row=part * piece, rows=piece)
+        add_sum(1, column=part * width, columns=width)
+    add_sum(2)
+    add_sum(3, gathered=True)
+    add_sum(4)
+    d_outer, d_inner, d_wo, d_window, d_pack = reduce_all(grads, sums, dp_size, ring_size, 7)
+    d_outer, d_inner, d_wo, d_pack = (
+        part.astype(wide) for part in (d_outer, d_inner, d_wo, d_pack)
+    )
+    weight_grads = []
+    for index in range(3):
+        pieces = []
+        for member in range(ring_size):
+            start = member * group - (member * group) // 128 * 128 + index * window
+            pieces.append(d_window[member, :, start : start + group])
+        weight_grads.append(jnp.concatenate(pieces, axis=1).astype(wide))
+    d_wq, d_wk, d_wv = weight_grads
+    d_bq, d_bv, d_bo, d_g1, d_s1, d_bu, d_g2, d_s2 = (d_pack[i, :piece] for i in range(8))
+    d_bi = d_pack[8]
     shape = (micro, row_count, block_tokens, width)
     return (
         output_low.reshape(shape),

time: 554 us -> 476 us (0.86)
  Pallas kernels: 430 us -> 350 us
  other arithmetic: 7.79 us -> 21.5 us
  local copies, waits for them, and re-layouts: 37.9 us -> 26 us
    pallas_call x2 -> x1, Pallas kernels: 74 us -> 19.4 us  [to_tokens(): pl.pallas_call(functools.partial(to_tokens_kernel, ring_size), out_shape=...]
    pallas_call x2 -> x1, Pallas kernels: 74.1 us -> 21.4 us  [to_heads(): pl.pallas_call(functools.partial(to_heads_kernel, ring_size), out_shape=j...]
    pallas_call x2 -> x3, Pallas kernels: 225 us -> 253 us  [the longest x1 117 us: reduce_all(): pl.pallas_call(functools.partial(reduce_kernel, items, ring_size), out_sh...]
    convert_element_type x2 -> x9, other arithmetic: 0.01 us -> 8.54 us  [the longest x4 4.56 us: fast_body(): part.astype(wide)]
    unnamed x106 -> x87, local copies, waits for them, and re-layouts: 13.2 us -> 5.29 us
    concatenate x2 -> x0, local copies, waits for them, and re-layouts: 6.19 us -> none  [the longest x1 6.18 us: fast_body(): jnp.concatenate(vectors)]
    dot_general x9 -> x3, matrix products: 17.2 us -> 12.9 us  [the longest x1 5.13 us: fast_body(): jnp.einsum('mtd,de->met', hidden_all, w_window, preferred_element_type=wide)]
where the time goes in v2:
time: 476 us; the launch traced here: 470 us
  Pallas kernels  350 us (74%)
  matrix products  70.9 us (15%)
  local copies, waits for them, and re-layouts  26 us (5%)
  other arithmetic  21.5 us (5%)
    pallas_call x1, Pallas kernels, reduce_all(): pl.pallas_call(functools.partial(reduce_kernel, items, ring_size), out_sh...  117 us
    pallas_call x1, Pallas kernels, gather_all(): pl.pallas_call(functools.partial(gather_kernel, items, ring_size), out_sh...  79.4 us
    pallas_call x1, Pallas kernels, scatter_line(): pl.pallas_call(functools.partial(scatter_line_kernel, ring_size), out_sha...  56.7 us
    pallas_call x1, Pallas kernels, attend_back(): pl.pallas_call(functools.partial(attend_back_kernel, score_scale, block),...  22.4 us
    pallas_call x1, Pallas kernels, to_heads(): pl.pallas_call(functools.partial(to_heads_kernel, ring_size), out_shape=j...  21.4 us
    pallas_call x1, Pallas kernels, attend(): pl.pallas_call(functools.partial(attend_kernel, score_scale, block), grid...  20.3 us
    pallas_call x1, Pallas kernels, to_tokens(): pl.pallas_call(functools.partial(to_tokens_kernel, ring_size), out_shape=...  19.4 us
    dot_general x1, matrix products, fast_body(): jnp.dot(first_low, w_inner, preferred_element_type=wide) + b_inner  18.7 us

profile of v2, /device:TPU:0, one launch (start us, length us, event | category | flops | bytes accessed | tf_op | source)
XLA Modules:
  0.0 469.7 jit_solution(12680850712408247945)
XLA Ops:
  5.3 79.4 %shard_map.347 = (bf16[768,768]{1,0:T(8,128)(2,1)}, bf16[128,384]{1,0:T(8,128)(2,1)}, s32[64,128]{1,0:T(8,128)}, bf16[256,768]{1,0:T(8,128)(2,1)}, bf16[768,768]...) custom-call(bf16[96,768]{1,0:T(8,128)(2,1)} %refs_0_.1, ...), custom_call_target="tpu_custom_call" | custom-call | tf_op jit(solution)/shard_map/pallas_call | solution.py:693
  86.7 5.1 %add_convert_fusion = bf16[768,2,1024]{2,0,1:T(8,128)(2,1)S(1)} fusion(f32[768]{0:T(1024)S(1)} %pad_maximum_fusion.1, bf16[2,1024,768]{2,1,0:T(8,128)(2,1)} %get-tuple-element.41, bf16[768,768]{1,0:T(8,128)(2,1)} %get-tuple-element.40), kind=kOutput, calls=%fused_computation.25 | convolution fusion | flops 2419064832 | bytes 7474176 | tf_op jit(solution)/shard_map/mtd,de->met/dot_general | solution.py:1421
  91.8 1.8 constant_dynamic-slice_fusion.1.qkv
  94.5 1.9 reshape_reshape.8.seg_col
  97.0 20.3 %shard_map.348 = (f32[2,3,64,1024]{3,2,1,0:T(8,128)}, bf16[2,3,64,1024]{3,2,1,0:T(8,128)(2,1)}, f32[2,3,2,1024]{3,2,1,0:T(2,128)}) custom-call(bf16[2,3,3,64,1024]{4,3,2,1,0:T(8,128)(2,1)} %constant_dynamic-slice_fusion.1.qkv, s32[2,1024,1]{2,1,0:T(8,128)} %reshape_reshape.8.seg_col, s32[2,1,1024]{2,1,0:T(1,128)} %reshape.292.seg_row), custom_call_target="tpu_custom_call" | custom-call | tf_op jit(solution)/shard_map/pallas_call | solution.py:1207
  117.3 19.4 %shard_map.349 = bf16[2,768,256]{2,1,0:T(8,128)(2,1)} custom-call(bf16[2,192,1024]{2,1,0:T(8,128)(2,1)} %bitcast.227), custom_call_target="tpu_custom_call" | custom-call | tf_op jit(solution)/shard_map/pallas_call | solution.py:799
  136.7 2.1 fusion.28
  139.8 18.7 %fusion.2 = (bf16[512,3072]{1,0:T(8,128)(2,1)S(1)}, f32[512,3072]{1,0:T(8,128)}) fusion(f32[3072]{0:T(1024)S(1)} %bitcast.243, bf16[768,3072]{1,0:T(8,128)(2,1)} %get-tuple-element.46, f32[512,768]{1,0:T(8,128)S(1)} %fusion.18, f32[768]{0:T(1024)S(1)} %add.170, f32[768]{0:T(1024)S(1)} %mul.159), kind=kOutput, calls=%fused_computation.4 | convolution fusion | flops 2520907776 | bytes 15747072 | tf_op jit(solution)/shard_map/dot_general | solution.py:1443
  158.6 6.2 %fusion.57 = (f32[512]{0:T(512)S(1)}, f32[512,768]{1,0:T(8,128)S(1)}) fusion(f32[768]{0:T(1024)S(1)} %add.175, bf16[512,3072]{1,0:T(8,128)(2,1)S(1)} %get-tuple-element.153, bf16[3072,768]{1,0:T(8,128)(2,1)} %get-tuple-element.47, f32[768]{0:T(1024)S(1)} %add.170, f32[512,768]{1,0:T(8,128)S(1)} %fusion.18, f32[768]{0:T(1024)S(1)} %mul.159), kind=kOutput, calls=%fused_computation.173 | convolution fusion | flops 2417884672 | bytes 11021312 | tf_op jit(solution)/shard_map/dot_general | solution.py:1445
  166.5 2.0 convolution_convert_fusion.4
  168.5 13.4 %shard_map.350 = bf16[8,32,768]{2,1,0:T(8,128)(2,1)} custom-call(bf16[32,768]{1,0:T(8,128)(2,1)} %bitcast.230), custom_call_target="tpu_custom_call" | custom-call | tf_op jit(solution)/shard_map/pallas_call | solution.py:843
  182.0 1.4 dynamic-slice_bitcast_fusion
  186.2 1.5 fusion.58
  192.6 1.4 constant_dynamic-slice_fusion
  194.9 2.2 fusion.32
  197.4 2.4 fusion.27
  201.7 4.8 %fusion.59 = (bf16[3072]{0:T(1024)(128)(2,1)S(1)}, bf16[512,3072]{1,0:T(8,128)(2,1)S(1)}) fusion(f32[512,3072]{1,0:T(8,128)S(1)} %bitcast.266, f32[3072]{0:T(1024)S(1)} %bitcast.244, bf16[3072,768]{1,0:T(8,128)(2,1)S(1)} %bitcast.264, f32[512,768]{1,0:T(8,128)S(1)} %get-tuple-element.119), kind=kOutput, calls=%fused_computation.175 | convolution fusion | flops 2435183616 | bytes 15747072 | tf_op jit(solution)/shard_map/nd,fd->nf/dot_general | solution.py:1494
  206.5 3.0 multiply_reduce_fusion.1
  209.6 1.6 fusion.54
  211.2 1.7 fusion.20.refs_0_
  212.9 21.4 %shard_map.351 = bf16[2,1,192,1024]{3,2,1,0:T(8,128)(2,1)} custom-call(bf16[2,768,256]{2,1,0:T(8,128)(2,1)} %fusion.20.refs_0_), custom_call_target="tpu_custom_call" | custom-call | tf_op jit(solution)/shard_map/pallas_call | solution.py:749
  234.2 22.4 %shard_map.352 = (bf16[2,3,64,1024]{3,2,1,0:T(8,128)(2,1)}, bf16[2,3,64,1024]{3,2,1,0:T(8,128)(2,1)}, bf16[2,3,64,1024]{3,2,1,0:T(8,128)(2,1)}) custom-call(bf16[2,3,3,64,1024]{4,3,2,1,0:T(8,128)(2,1)} %constant_dynamic-slice_fusion.1.qkv, s32[2,1024,1]{2,1,0:T(8,128)} %reshape_reshape.8.seg_col, s32[2,1,1024]{2,1,0:T(1,128)} %reshape.292.seg_row, ...), custom_call_target="tpu_custom_call" | custom-call | tf_op jit(solution)/shard_map/pallas_call | solution.py:1259
  259.5 4.1 convolution_convert_fusion.2
  263.6 56.7 %shard_map.353 = f32[2,256,768]{2,1,0:T(8,128)} custom-call(bf16[2,4,256,768]{3,2,1,0:T(8,128)(2,1)} %bitcast.215), custom_call_target="tpu_custom_call" | custom-call | tf_op jit(solution)/shard_map/pallas_call | solution.py:1163
  320.3 3.0 fusion.26
  323.3 6.8 %convolution_convert_fusion.1.refs_0_ = bf16[3072,768]{1,0:T(8,128)(2,1)} fusion(bf16[512,3072]{1,0:T(8,128)(2,1)} %copy-done.29, f32[512,768]{1,0:T(8,128)S(1)} %copy-done.6), kind=kOutput, calls=%fused_computation.29 | convolution fusion | flops 2418671616 | bytes 9437184 | tf_op jit(solution)/shard_map/nf,nd->fd/dot_general | solution.py:1491
  330.2 4.6 convolution_convert_fusion.refs_1_
  334.8 1.8 bitcast_convert_fusion.1.refs_2_
  337.1 3.7 bitcast_convert_fusion.refs_3_
  343.0 116.9 %shard_map.354 = (bf16[384,768]{1,0:T(8,128)(2,1)}, bf16[96,3072]{1,0:T(8,128)(2,1)}, bf16[96,768]{1,0:T(8,128)(2,1)}, bf16[4,96,768]{2,1,0:T(8,128)(2,1)}, bf16[16,384]{1,0:T(8,128)(2,1)}) custom-call(bf16[3072,768]{1,0:T(8,128)(2,1)} %convolution_convert_fusion.1.refs_0_, bf16[768,3072]{1,0:T(8,128)(2,1)} %convolution_convert_fusion.refs_1_, ...), custom_call_target="tpu_custom_call" | custom-call | tf_op jit(solution)/shard_map/pallas_call | solution.py:1060
  460.0 1.4 slice_bitcast_fusion.3
  463.9 1.6 convert_element_type.181
  (168 shorter events, 33.7 us)
Async XLA Ops:
  86.4 53.4 %copy-start.17 = (f32[8,1,384]{2,1,0:T(1,128)}, f32[8,1,384]{2,1,0:T(1,128)S(1)}, u32[]{:S(2)}) copy-start(f32[8,1,384]{2,1,0:T(1,128)S(1)} %slice_convert_fusion) | copy-start | bytes 36868
  93.6 43.1 %copy-start = (bf16[2,1,256,768]{3,2,1,0:T(8,128)(2,1)S(1)}, bf16[2,1,256,768]{3,2,1,0:T(8,128)(2,1)}, u32[]{:S(2)}) copy-start(bf16[2,1,256,768]{3,2,1,0:T(8,128)(2,1)} %param.20) | copy-start | bytes 2359300
  93.6 43.1 %copy-start.25 = (bf16[768,768]{1,0:T(8,128)(2,1)S(1)}, bf16[768,768]{1,0:T(8,128)(2,1)}, u32[]{:S(2)}) copy-start(bf16[768,768]{1,0:T(8,128)(2,1)} %get-tuple-element.45) | copy-start | bytes 3538948
  139.3 19.2 %copy-start.13 = (f32[1,2,2,128]{3,1,2,0:T(2,128)}, f32[1,2,2,128]{3,1,2,0:T(2,128)S(1)}, u32[]{:S(2)}) copy-start(f32[1,2,2,128]{3,1,2,0:T(2,128)S(1)} %copy.84) | copy-start | bytes 6148
  139.7 69.9 %copy-start.1 = (f32[512,768]{1,0:T(8,128)}, f32[512,768]{1,0:T(8,128)S(1)}, u32[]{:S(2)}) copy-start(f32[512,768]{1,0:T(8,128)S(1)} %fusion.18) | copy-start | bytes 4718596
  139.7 18.8 %copy-start.21 = (f32[768]{0:T(1024)}, f32[768]{0:T(1024)S(1)}, u32[]{:S(2)}) copy-start(f32[768]{0:T(1024)S(1)} %add.170) | copy-start | bytes 9220
  139.8 18.8 %copy-start.15 = (f32[768]{0:T(1024)}, f32[768]{0:T(1024)S(1)}, u32[]{:S(2)}) copy-start(f32[768]{0:T(1024)S(1)} %mul.159) | copy-start | bytes 9220
  158.6 6.2 %copy-start.29 = (bf16[512,3072]{1,0:T(8,128)(2,1)}, bf16[512,3072]{1,0:T(8,128)(2,1)S(1)}, u32[]{:S(2)}) copy-start(bf16[512,3072]{1,0:T(8,128)(2,1)S(1)} %get-tuple-element.153) | copy-start | bytes 9437188
  164.8 1.7 copy-start.20
  166.5 16.8 %copy-start.19 = (pred[2,256]{1,0:T(4,128)(4,1)}, pred[2,256]{1,0:T(4,128)(4,1)S(1)}, u32[]{:S(2)}) copy-start(pred[2,256]{1,0:T(4,128)(4,1)S(1)} %fusion.50) | copy-start | bytes 1540
  192.6 7.2 %copy-start.4 = (bf16[2,1,256,768]{3,2,1,0:T(8,128)(2,1)S(1)}, bf16[2,1,256,768]{3,2,1,0:T(8,128)(2,1)}, u32[]{:S(2)}) copy-start(bf16[2,1,256,768]{3,2,1,0:T(8,128)(2,1)} %param.24) | copy-start | bytes 2359300
  194.9 6.3 %slice-start.4 = ((s8[6291456]{0:T(1024)(128)(4,1)}), s8[4194304]{0:T(1024)(128)(4,1)S(1)}, s32[]{:S(2)}) async-start(s8[6291456]{0:T(1024)(128)(4,1)} %bitcast.265), calls=%async_computation.4 | async-start | bytes 8388608
  197.4 3.8 slice-start.2
  199.9 1.3 slice-start.3
  199.9 1.8 slice-start.5
  200.6 5.8 %slice-start = ((s8[4718592]{0:T(1024)(128)(4,1)}), s8[4194304]{0:T(1024)(128)(4,1)S(1)}, s32[]{:S(2)}) async-start(s8[4718592]{0:T(1024)(128)(4,1)} %bitcast.261), calls=%async_computation | async-start | bytes 8388608
  201.2 5.2 %copy-start.5 = (f32[512,768]{1,0:T(8,128)}, f32[512,768]{1,0:T(8,128)S(1)}, u32[]{:S(2)}) copy-start(f32[512,768]{1,0:T(8,128)S(1)} %get-tuple-element.119) | copy-start | bytes 4718596
  201.7 4.8 %copy-start.16 = (f32[768]{0:T(1024)S(1)}, f32[768]{0:T(1024)}, u32[]{:S(2)}) copy-start(f32[768]{0:T(1024)} %copy-done.15) | copy-start | bytes 9220
  201.7 4.8 %slice-start.1 = ((s8[4718592]{0:T(1024)(128)(4,1)}), s8[524288]{0:T(1024)(128)(4,1)S(1)}, s32[]{:S(2)}) async-start(s8[4718592]{0:T(1024)(128)(4,1)} %bitcast.261), calls=%async_computation.1 | async-start | bytes 1048576
  206.5 3.1 copy-start.27
  206.5 3.1 copy-start.14
  209.6 1.6 copy-start.26
  256.6 1.4 copy-start.8
  256.6 1.6 copy-start.9
  320.3 3.0 copy-start.6
  323.3 6.9 %copy-start.2 = (f32[512,768]{1,0:T(8,128)S(1)}, f32[512,768]{1,0:T(8,128)}, u32[]{:S(2)}) copy-start(f32[512,768]{1,0:T(8,128)} %copy-done.1) | copy-start | bytes 4718596
  323.3 6.9 %copy-start.22 = (f32[768]{0:T(1024)S(1)}, f32[768]{0:T(1024)}, u32[]{:S(2)}) copy-start(f32[768]{0:T(1024)} %copy-done.21) | copy-start | bytes 9220
  323.3 6.9 %copy-start.28 = (bf16[512,3072]{1,0:T(8,128)(2,1)S(1)}, bf16[512,3072]{1,0:T(8,128)(2,1)}, u32[]{:S(2)}) copy-start(bf16[512,3072]{1,0:T(8,128)(2,1)} %copy-done.27) | copy-start | bytes 9437188
  330.2 4.6 copy-start.10
  334.8 2.3 copy-start.23
  460.0 6.8 %copy-start.12 = (bf16[96,3072]{1,0:T(8,128)(2,1)S(1)}, bf16[96,3072]{1,0:T(8,128)(2,1)}, u32[]{:S(2)}) copy-start(bf16[96,3072]{1,0:T(8,128)(2,1)} %get-tuple-element.58) | copy-start | bytes 1769476
  460.0 8.5 %copy-start.11 = (bf16[384,768]{1,0:T(8,128)(2,1)S(1)}, bf16[384,768]{1,0:T(8,128)(2,1)}, u32[]{:S(2)}) copy-start(bf16[384,768]{1,0:T(8,128)(2,1)} %get-tuple-element.59) | copy-start | bytes 1769476
  (4 other events, 4.2 us)
